TPU v7x, 256 devices: a whole 4x4x8 slice. The times are simulated.
256 devices in a mesh: slab: 4 (over y), inner: 64 (over x, z, core).
Axes of the slice: x: 4, y: 4, z: 8, core: 2. Of those that a mesh axis runs over, the one named last changes fastest.
Arguments:
- expression: float32 [16384, 4096], P('slab', 'inner'), may hold values from -6 to 6
- cell_tiles: bfloat16 [64, 3, 256, 256], P('slab'), may hold values from -0.109375 to 0.109375
- cell_blocks: int32 [64, 3], P('slab'), may hold values from 0 to 63, as said below
- cell_counts: int32 [64], P('slab'), may hold values from 2 to 3, as said below
- gene_tiles: bfloat16 [32, 3, 128, 128], replicated, may hold values from -0.15625 to 0.15625
- gene_blocks: int32 [32, 3], replicated, may hold values from 0 to 31
Outputs:
- lowrank: float32 [16384, 4096], P('slab', 'inner')
Inputs may be any that keep to these rules, and one draw needn't show every extreme that they name: `cell_blocks`: row block b lists b first, then b - 1 (1 for b = 0), then a block at most 2 above b (below b when that passes the last block). `cell_counts`: each cell row block uses its first 2 or 3 listed tiles.
All inputs are finite; a program needn't handle non-finite values.
Results may differ from a plain program's by a relative error of at most 0.002.
Values may be sent and summed in bfloat16 or wider, within the bound.
No kernel may reach another device: no remote copies, remote signals or barrier semaphores. Data moves between devices by JAX's collectives and lax.ppermute only.
A program may use at most 128 MiB of HBM per device.

v0:
```python
import jax
import jax.numpy as jnp
from jax import lax
from jax.sharding import PartitionSpec as P

GENES = 4096
GT = 128
REACH = 2
STEPS = 2
GB = 32


shrink = 0.5


def extended(cells, sides, width):
    for axis, dim in sides:
        count = lax.axis_size(axis)
        ends = count - 1
        head = lax.slice_in_dim(cells, 0, width, axis=dim)
        tail = lax.slice_in_dim(cells, cells.shape[dim] - width, cells.shape[dim], axis=dim)
        cells = jnp.concatenate(
            [
                lax.ppermute(tail, axis, [(i, (i + 1) % count) for i in range(ends)]),
                cells,
                lax.ppermute(head, axis, [((i + 1) % count, i) for i in range(ends)]),
            ],
            axis=dim,
        )
    return cells


def gene_product(lowp_rows, gene_tiles, gene_blocks):
    row_count = lowp_rows.shape[0]
    stacked = lowp_rows.reshape(row_count, GB, GT)
    gathered = stacked[:, gene_blocks]
    total = jnp.einsum("cakh,akhj->caj", gathered, gene_tiles, preferred_element_type=jnp.float32)
    return total.reshape(row_count, GENES)


def cell_product(lowp_group, cell_tiles, local_index, slot_mask):
    block_rows = cell_tiles.shape[2]
    group_rows, local_genes = lowp_group.shape
    padded = extended(lowp_group, (("slab", 0),), REACH * block_rows)
    stacked = padded.reshape(-1, block_rows, local_genes)
    gathered = stacked[local_index] * slot_mask[:, :, None, None]
    total = jnp.einsum("bkij,bkjg->big", cell_tiles, gathered, preferred_element_type=jnp.float32)
    return total.reshape(group_rows, local_genes)


def proximal(moved, expression):
    offset = moved - expression
    return expression + jnp.sign(offset) * jnp.maximum(jnp.abs(offset) - shrink, 0.0)


def local(expression, cell_tiles, cell_blocks, cell_counts, gene_tiles, gene_blocks):
    parts_inner = lax.axis_size("inner")
    group_rows, local_genes = expression.shape
    per_device = group_rows // parts_inner
    local_blocks = cell_tiles.shape[0]
    slot_total = cell_tiles.shape[1]
    first_block = lax.axis_index("slab") * local_blocks
    local_index = cell_blocks - first_block + REACH
    slot_mask = (jnp.arange(slot_total, dtype=jnp.int32)[None, :] < cell_counts[:, None]).astype(
        jnp.bfloat16
    )
    row_expression = lax.all_to_all(
        expression.reshape(parts_inner, per_device, local_genes),
        "inner",
        split_axis=0,
        concat_axis=2,
        tiled=True,
    )
    row_expression = row_expression.reshape(per_device, GENES)
    current = row_expression
    for step in range(STEPS):
        lowp = current.astype(jnp.bfloat16)
        geneterm = gene_product(lowp, gene_tiles, gene_blocks)
        lowp_group = lax.all_to_all(
            lowp.reshape(1, per_device, GENES), "inner", split_axis=2, concat_axis=0, tiled=True
        )
        lowp_group = lowp_group.reshape(group_rows, local_genes)
        cell_group = cell_product(lowp_group, cell_tiles, local_index, slot_mask)
        cellterm = lax.all_to_all(
            cell_group.reshape(parts_inner, per_device, local_genes),
            "inner",
            split_axis=0,
            concat_axis=2,
            tiled=True,
        )
        cellterm = cellterm.reshape(per_device, GENES)
        moved = current - (cellterm + geneterm)
        current = proximal(moved, row_expression)
    result = lax.all_to_all(
        current.reshape(1, per_device, GENES), "inner", split_axis=2, concat_axis=0, tiled=True
    )
    return result.reshape(group_rows, local_genes)


def solution(mesh):
    in_specs = (
        P("slab", "inner"),
        P("slab", None, None, None),
        P("slab", None),
        P("slab"),
        P(),
        P(),
    )
    out_specs = P("slab", "inner")
    return jax.shard_map(local, mesh=mesh, in_specs=in_specs, out_specs=out_specs, check_vma=False)
```

profile of v0, /device:TPU:32, one launch (start us, length us, event | category | flops | bytes accessed | tf_op | source)
XLA Modules:
  0.0 475.3 jit_solution(4227695632068150133)
XLA Ops:
  0.0 3.3 copy.74
  3.3 3.4 reshape.278
  6.8 40.1 %all_to_all.90 = f32[64,1,4096]{2,1,0:T(1,128)} all-to-all(f32[64,1,4096]{2,1,0:T(1,128)} %reshape.278), channel_id=1, replica_groups=mesh['slab'=4,'inner'=64] {'inner'}, dimensions={0} | all-to-all | bytes 2097152 | tf_op jit(solution)/shard_map/all_to_all | solution.py:67
  47.4 5.3 %reduce = f32[64,4096]{1,0:T(8,128)} reduce(f32[64,1,4096]{2,1,0:T(1,128)} %all_to_all.90, f32[]{:T(128)} %broadcast.111), dimensions={1}, to_apply=%all_to_all.66.reduce_sub_computation | reduce | bytes 2097156 | tf_op jit(solution)/shard_map/all_to_all | solution.py:67
  55.8 4.2 copy.75
  64.9 5.4 %copy.76 = bf16[1,64,4096]{1,0,2:T(2,128)(2,1)} copy(bf16[1,64,4096]{2,1,0:T(8,128)(2,1)} %convert_element_type.33) | data formatting | bytes 1048576 | tf_op jit(solution)/shard_map/convert_element_type | solution.py:77
  70.8 24.4 %reduce.1 = bf16[4096,64]{1,0:T(8,128)(2,1)} reduce(bf16[4096,1,64]{2,1,0:T(2,128)(2,1)} %bitcast.122, bf16[]{:T(256)} %broadcast.112), dimensions={1}, to_apply=%bitcast.90.reduce_sub_computation | reduce | bytes 1048578
  95.2 3.2 reshape.280
  98.4 7.1 %all-to-all-start.1 = ((bf16[64,2,2048]{2,1,0:T(2,128)(2,1)}), bf16[64,2,2048]{2,1,0:T(2,128)(2,1)}, u32[]{:S(2)}, u32[]{:S(2)}) async-start(bf16[64,2,2048]{2,1,0:T(2,128)(2,1)} %reshape.280), calls=%async_computation.1 | async-start | bytes 1048576 | tf_op jit(solution)/shard_map/all_to_all | solution.py:79
  105.7 16.7 %all-to-all-done.1 = bf16[64,2,2048]{2,1,0:T(2,128)(2,1)} async-done(((bf16[64,2,2048]{2,1,0:T(2,128)(2,1)}), bf16[64,2,2048]{2,1,0:T(2,128)(2,1)}, u32[]{:S(2)}, u32[]{:S(2)}) %all-to-all-start.1) | async-done | bytes 524320 | tf_op jit(solution)/shard_map/all_to_all | solution.py:79
  122.5 5.6 %reshape.281 = bf16[4096,1,64]{2,1,0:T(2,128)(2,1)} reshape(bf16[64,2,2048]{2,1,0:T(2,128)(2,1)} %all-to-all-done.1) | data formatting | bytes 1048576
  128.1 5.2 %copy.77 = bf16[1,64,4096]{2,1,0:T(8,128)(2,1)} copy(bf16[1,64,4096]{1,0,2:T(2,128)(2,1)} %bitcast.120) | data formatting | bytes 1048576 | tf_op jit(solution)/shard_map/all_to_all | solution.py:79
  137.3 3.5 collective-permute-start
  142.4 4.0 copy.79
  154.1 5.3 %fusion.4 = f32[16,256,64]{1,2,0:T(8,128)S(1)} fusion(bf16[16,3,256,256]{3,2,1,0:T(8,128)(2,1)} %param.7, bf16[16,3,256,64]{2,3,1,0:T(8,128)(2,1)} %bitcast.117, bf16[16,3]{1,0:T(8,128)(2,1)S(1)} %fusion.12), kind=kOutput, calls=%fused_computation.10 | convolution fusion | flops 403439616 | bytes 8912992 | tf_op jit(solution)/shard_map/bkij,bkjg->big/dot_general | solution.py:47
  163.6 4.1 copy.129
  167.8 3.5 reshape.282
  171.2 6.7 %all-to-all-start.2 = ((f32[64,1,4096]{2,1,0:T(1,128)}), f32[64,1,4096]{2,1,0:T(1,128)}, u32[]{:S(2)}, u32[]{:S(2)}) async-start(f32[64,1,4096]{2,1,0:T(1,128)} %reshape.282), calls=%async_computation.2 | async-start | bytes 2097152 | tf_op jit(solution)/shard_map/all_to_all | solution.py:84
  186.4 19.4 %all-to-all-done.2 = f32[64,1,4096]{2,1,0:T(1,128)} async-done(((f32[64,1,4096]{2,1,0:T(1,128)}), f32[64,1,4096]{2,1,0:T(1,128)}, u32[]{:S(2)}, u32[]{:S(2)}) %all-to-all-start.2) | async-done | bytes 1048608 | tf_op jit(solution)/shard_map/all_to_all | solution.py:84
  205.7 5.3 %reduce.2 = f32[64,4096]{1,0:T(8,128)} reduce(f32[64,1,4096]{2,1,0:T(1,128)} %all-to-all-done.2, f32[]{:T(128)} %broadcast.111), dimensions={1}, to_apply=%all_to_all.72.reduce_sub_computation | reduce | bytes 2097156 | tf_op jit(solution)/shard_map/all_to_all | solution.py:84
  211.1 3.1 reshape.283
  214.2 3.2 copy.100
  217.4 4.2 add_convert_fusion
  225.5 3.2 copy.112
  228.7 3.2 fusion.13
  231.9 5.3 %copy.90 = bf16[1,64,4096]{1,0,2:T(2,128)(2,1)} copy(bf16[1,64,4096]{2,1,0:T(8,128)(2,1)} %fusion.13) | data formatting | bytes 1048576 | tf_op jit(solution)/shard_map/convert_element_type | solution.py:77
  237.2 24.8 %reduce.3 = bf16[4096,64]{1,0:T(8,128)(2,1)} reduce(bf16[4096,1,64]{2,1,0:T(2,128)(2,1)} %bitcast.123, bf16[]{:T(256)} %broadcast.112), dimensions={1}, to_apply=%bitcast.94.reduce_sub_computation | reduce | bytes 1048578
  265.1 24.1 %all_to_all.91 = bf16[64,2,2048]{2,1,0:T(2,128)(2,1)} all-to-all(bf16[64,2,2048]{2,1,0:T(2,128)(2,1)} %reshape.284), channel_id=1, replica_groups=mesh['slab'=4,'inner'=64] {'inner'}, dimensions={0} | all-to-all | bytes 1048576 | tf_op jit(solution)/shard_map/all_to_all | solution.py:79
  289.1 5.5 %reshape.285 = bf16[4096,1,64]{2,1,0:T(2,128)(2,1)} reshape(bf16[64,2,2048]{2,1,0:T(2,128)(2,1)} %all_to_all.91) | data formatting | bytes 1048576
  294.7 5.2 %copy.91 = bf16[1,64,4096]{2,1,0:T(8,128)(2,1)} copy(bf16[1,64,4096]{1,0,2:T(2,128)(2,1)} %bitcast.121) | data formatting | bytes 1048576 | tf_op jit(solution)/shard_map/all_to_all | solution.py:79
  304.0 4.6 collective-permute-start.2
  310.1 4.2 copy.93
  322.0 5.3 %fusion.7 = f32[16,256,64]{1,2,0:T(8,128)S(1)} fusion(bf16[16,3,256,256]{3,2,1,0:T(8,128)(2,1)} %param.7, bf16[16,3,256,64]{2,3,1,0:T(8,128)(2,1)} %bitcast.116, bf16[16,3]{1,0:T(8,128)(2,1)S(1)} %fusion.12), kind=kOutput, calls=%fused_computation.11 | convolution fusion | flops 403439616 | bytes 8912992 | tf_op jit(solution)/shard_map/bkij,bkjg->big/dot_general | solution.py:47
  331.6 4.1 copy.128
  335.7 3.4 reshape.286
  339.2 7.1 %all-to-all-start.4 = ((f32[64,1,4096]{2,1,0:T(1,128)}), f32[64,1,4096]{2,1,0:T(1,128)}, u32[]{:S(2)}, u32[]{:S(2)}) async-start(f32[64,1,4096]{2,1,0:T(1,128)} %reshape.286), calls=%async_computation.4 | async-start | bytes 2097152 | tf_op jit(solution)/shard_map/all_to_all | solution.py:84
  355.4 18.5 %all-to-all-done.4 = f32[64,1,4096]{2,1,0:T(1,128)} async-done(((f32[64,1,4096]{2,1,0:T(1,128)}), f32[64,1,4096]{2,1,0:T(1,128)}, u32[]{:S(2)}, u32[]{:S(2)}) %all-to-all-start.4) | async-done | bytes 1048608 | tf_op jit(solution)/shard_map/all_to_all | solution.py:84
  373.8 5.4 %reduce.4 = f32[64,4096]{1,0:T(8,128)} reduce(f32[64,1,4096]{2,1,0:T(1,128)} %all-to-all-done.4, f32[]{:T(128)} %broadcast.111), dimensions={1}, to_apply=%all_to_all.78.reduce_sub_computation | reduce | bytes 2097156 | tf_op jit(solution)/shard_map/all_to_all | solution.py:84
  382.3 3.2 copy.113
  385.5 4.5 multiply_add_fusion
  390.0 5.3 %copy.105 = f32[1,64,4096]{1,0,2:T(1,128)} copy(f32[1,64,4096]{2,1,0:T(8,128)} %multiply_add_fusion) | data formatting | bytes 2097152 | tf_op jit(solution)/shard_map/add | solution.py:53
  395.3 20.3 %reduce.5 = f32[4096,64]{1,0:T(8,128)} reduce(f32[4096,1,64]{2,1,0:T(1,128)} %bitcast.129, f32[]{:T(128)} %broadcast.111), dimensions={1}, to_apply=%bitcast.98.reduce_sub_computation | reduce | bytes 2097156
  415.6 3.7 reshape.288
  419.3 34.9 %all_to_all.92 = f32[64,1,4096]{2,1,0:T(1,128)} all-to-all(f32[64,1,4096]{2,1,0:T(1,128)} %reshape.288), channel_id=1, replica_groups=mesh['slab'=4,'inner'=64] {'inner'}, dimensions={0} | all-to-all | bytes 2097152 | tf_op jit(solution)/shard_map/all_to_all | solution.py:94
  454.2 5.3 %reduce.6 = f32[64,4096]{1,0:T(8,128)} reduce(f32[64,1,4096]{2,1,0:T(1,128)} %all_to_all.92, f32[]{:T(128)} %broadcast.111), dimensions={1}, to_apply=%all_to_all.81.reduce_sub_computation | reduce | bytes 2097156 | tf_op jit(solution)/shard_map/all_to_all | solution.py:94
  459.5 4.7 reshape.289
  464.2 3.8 copy.116
  468.0 4.2 copy.107
  (64 shorter events, 75.1 us)
Async XLA Ops:
  0.0 217.4 %copy-start = (bf16[32,3,128,128]{3,2,1,0:T(8,128)(2,1)S(1)}, bf16[32,3,128,128]{3,2,1,0:T(8,128)(2,1)}, u32[]{:S(2)}) copy-start(bf16[32,3,128,128]{3,2,1,0:T(8,128)(2,1)} %param.10) | copy-start | bytes 9437188
  95.2 10.2 %copy-start.1 = (s32[16,3]{0,1:T(4,128)S(1)}, s32[16,3]{0,1:T(4,128)}, u32[]{:S(2)}) copy-start(s32[16,3]{0,1:T(4,128)} %param.8) | copy-start | bytes 580
  95.2 10.4 %copy-start.3 = (s32[16]{0:T(128)S(1)}, s32[16]{0:T(128)}, u32[]{:S(2)}) copy-start(s32[16]{0:T(128)} %param.9) | copy-start | bytes 196
  98.4 24.1 %all-to-all-start.1 = ((bf16[64,2,2048]{2,1,0:T(2,128)(2,1)}), bf16[64,2,2048]{2,1,0:T(2,128)(2,1)}, u32[]{:S(2)}, u32[]{:S(2)}) async-start(bf16[64,2,2048]{2,1,0:T(2,128)(2,1)} %reshape.280), calls=%async_computation.1 | async-start | bytes 1048576 | tf_op jit(solution)/shard_map/all_to_all | solution.py:79
  137.3 11.8 %collective-permute-start = (bf16[512,64]{0,1:T(8,128)(2,1)S(1)}, bf16[512,64]{0,1:T(8,128)(2,1)S(1)}, u32[]{:S(2)}, u32[]{:S(2)}) collective-permute-start(bf16[512,64]{0,1:T(8,128)(2,1)S(1)} %slice.25), channel_id=1, source_target_pairs={{0,64},{64,128},{128,192},{1,65},{65,129},{129,193},{2,66},{66,130... | collective-permute-start | bytes 196616 | tf_op jit(solution)/shard_map/ppermute | solution.py:24
  141.1 8.0 %collective-permute-start.1 = (bf16[512,64]{0,1:T(8,128)(2,1)S(1)}, bf16[512,64]{0,1:T(8,128)(2,1)S(1)}, u32[]{:S(2)}, u32[]{:S(2)}) collective-permute-start(bf16[512,64]{0,1:T(8,128)(2,1)S(1)} %slice.27), channel_id=1, source_target_pairs={{64,0},{128,64},{192,128},{65,1},{129,65},{193,129},{66,2},{130,66... | collective-permute-start | bytes 196616 | tf_op jit(solution)/shard_map/ppermute | solution.py:26
  167.8 10.2 %copy-start.2 = (s32[32,3]{0,1:T(4,128)S(1)}, s32[32,3]{0,1:T(4,128)}, u32[]{:S(2)}) copy-start(s32[32,3]{0,1:T(4,128)} %param.11) | copy-start | bytes 1156
  171.2 34.5 %all-to-all-start.2 = ((f32[64,1,4096]{2,1,0:T(1,128)}), f32[64,1,4096]{2,1,0:T(1,128)}, u32[]{:S(2)}, u32[]{:S(2)}) async-start(f32[64,1,4096]{2,1,0:T(1,128)} %reshape.282), calls=%async_computation.2 | async-start | bytes 2097152 | tf_op jit(solution)/shard_map/all_to_all | solution.py:84
  304.0 13.1 %collective-permute-start.2 = (bf16[512,64]{0,1:T(8,128)(2,1)S(1)}, bf16[512,64]{0,1:T(8,128)(2,1)S(1)}, u32[]{:S(2)}, u32[]{:S(2)}) collective-permute-start(bf16[512,64]{0,1:T(8,128)(2,1)S(1)} %slice.29), channel_id=1, source_target_pairs={{0,64},{64,128},{128,192},{1,65},{65,129},{129,193},{2,66},{66,130... | collective-permute-start | bytes 196616 | tf_op jit(solution)/shard_map/ppermute | solution.py:24
  308.8 8.2 %collective-permute-start.3 = (bf16[512,64]{0,1:T(8,128)(2,1)S(1)}, bf16[512,64]{0,1:T(8,128)(2,1)S(1)}, u32[]{:S(2)}, u32[]{:S(2)}) collective-permute-start(bf16[512,64]{0,1:T(8,128)(2,1)S(1)} %slice.31), channel_id=1, source_target_pairs={{64,0},{128,64},{192,128},{65,1},{129,65},{193,129},{66,2},{130,66... | collective-permute-start | bytes 196616 | tf_op jit(solution)/shard_map/ppermute | solution.py:26
  339.2 34.7 %all-to-all-start.4 = ((f32[64,1,4096]{2,1,0:T(1,128)}), f32[64,1,4096]{2,1,0:T(1,128)}, u32[]{:S(2)}, u32[]{:S(2)}) async-start(f32[64,1,4096]{2,1,0:T(1,128)} %reshape.286), calls=%async_computation.4 | async-start | bytes 2097152 | tf_op jit(solution)/shard_map/all_to_all | solution.py:84
where the time goes:
time: 484 us; the launch traced here: 475 us
  local copies, waits for them, and re-layouts  170 us (35%)
  other arithmetic  103 us (21%)
  blocking collectives  99 us (20%)
  waiting for transfers between devices  54.6 us (11%)
  starting transfers between devices  31.5 us (7%)
  matrix products  16.9 us (3%)
    unnamed x3, other arithmetic  69.6 us
    unnamed x22, local copies, waits for them, and re-layouts  49.2 us
    all_to_all x1, blocking collectives, local(): lax.all_to_all(expression.reshape(parts_inner, per_device, local_genes),...  40.1 us
    all_to_all x2, waiting for transfers between devices, local(): lax.all_to_all(cell_group.reshape(parts_inner, per_device, local_genes),...  37.8 us
    all_to_all x1, blocking collectives, local(): lax.all_to_all(current.reshape(1, per_device, GENES), 'inner', split_axis...  34.9 us
    all_to_all x6, local copies, waits for them, and re-layouts, local(): lax.all_to_all(lowp.reshape(1, per_device, GENES), 'inner', split_axis=2,...  24.1 us
    all_to_all x1, blocking collectives, local(): lax.all_to_all(lowp.reshape(1, per_device, GENES), 'inner', split_axis=2,...  24.1 us
    all_to_all x1, waiting for transfers between devices, local(): lax.all_to_all(lowp.reshape(1, per_device, GENES), 'inner', split_axis=2,...  16.7 us
  transfers between devices with their start and end apart: 7, of which 3 were waited for; matrix products, arithmetic and copies ran while one was open for 7% of the time, Pallas kernels for 0%

commit v1 on v0

v1 whole, which is shorter than its diff:
```python
import jax
import jax.numpy as jnp
from jax import lax
from jax.experimental import pallas as pl
from jax.experimental.pallas import tpu as pltpu
from jax.sharding import Mesh
from jax.sharding import PartitionSpec as P

CHIPS = 32
OWN = 64
CHUNK = 128
BLOCKS = 16
CT = 256
GB = 32
GT = 128
SLOTS = 3
BEFORE, AFTER = 1, 2
HALF = 0.5

VMEM = pl.BlockSpec(memory_space=pltpu.VMEM)
SMEM = pl.BlockSpec(memory_space=pltpu.SMEM)
CHUNKED = (CHIPS, OWN, CHUNK)
DIMS_NT = (((1,), (1,)), ((), ()))


def soft(v):
    return v - jnp.clip(v, -HALF, HALF)


def params(mib):
    return pltpu.CompilerParams(vmem_limit_bytes=mib << 20)


def cost(flops, moved):
    return pl.CostEstimate(flops=flops, bytes_accessed=moved, transcendentals=0)


def cast_kernel(x_ref, low_ref):
    for j in range(CHIPS):
        low_ref[j] = x_ref[:, j * CHUNK : (j + 1) * CHUNK].astype(jnp.bfloat16)


def cast_chunks(x):
    return pl.pallas_call(
        cast_kernel,
        out_shape=jax.ShapeDtypeStruct(CHUNKED, jnp.bfloat16),
        in_specs=[VMEM],
        out_specs=VMEM,
        compiler_params=params(8),
        cost_estimate=cost(1 << 18, 3 << 19),
        name="cast_chunks",
    )(x)


def step_kernel(x_ref, d_ref, low_ref):
    for j in range(CHIPS):
        moved = x_ref[:, j * CHUNK : (j + 1) * CHUNK] - d_ref[j].astype(jnp.float32)
        low_ref[j] = moved.astype(jnp.bfloat16)


def step_chunks(x, d):
    return pl.pallas_call(
        step_kernel,
        out_shape=jax.ShapeDtypeStruct(CHUNKED, jnp.bfloat16),
        in_specs=[VMEM, VMEM],
        out_specs=VMEM,
        compiler_params=params(8),
        cost_estimate=cost(1 << 18, 2 << 20),
        name="step_chunks",
    )(x, d)


CELL_STEP = 4


def cell_kernel(blocks_ref, counts_ref, before_ref, low_ref, after_ref, tiles_ref, out_ref, all_ref):
    step = pl.program_id(0)
    first = lax.axis_index("slab") * BLOCKS - BEFORE

    @pl.when(step == 0)
    def _():
        all_ref[: 2 * BEFORE] = before_ref[...]
        all_ref[2 * BEFORE : 2 * BEFORE + CHIPS] = low_ref[...]
        all_ref[2 * BEFORE + CHIPS :] = after_ref[...]

    for i in range(CELL_STEP):
        b = step * CELL_STEP + i
        total = jnp.zeros((OWN, CT), jnp.float32)
        for k in range(SLOTS):
            at = 2 * (blocks_ref[k, b] - first)
            source = jnp.concatenate([all_ref[at], all_ref[at + 1]], axis=1)
            part = lax.dot_general(source, tiles_ref[i, k], DIMS_NT, preferred_element_type=jnp.float32)
            used = jnp.where(k < counts_ref[b], 1.0, 0.0).astype(jnp.float32)
            total = total + used * part
        out_ref[2 * i] = total[:, :CHUNK].astype(out_ref.dtype)
        out_ref[2 * i + 1] = total[:, CHUNK:].astype(out_ref.dtype)


def cell_product(blocks, counts, before, low, after, tiles, dtype):
    return pl.pallas_call(
        cell_kernel,
        grid=(BLOCKS // CELL_STEP,),
        out_shape=jax.ShapeDtypeStruct(CHUNKED, dtype),
        in_specs=[
            SMEM,
            SMEM,
            VMEM,
            VMEM,
            VMEM,
            pl.BlockSpec((CELL_STEP, SLOTS, CT, CT), lambda s: (s, 0, 0, 0)),
        ],
        out_specs=pl.BlockSpec((2 * CELL_STEP, OWN, CHUNK), lambda s: (s, 0, 0)),
        scratch_shapes=[pltpu.VMEM((CHIPS + 2 * (BEFORE + AFTER), OWN, CHUNK), jnp.bfloat16)],
        compiler_params=params(16),
        cost_estimate=cost(2 * BLOCKS * SLOTS * CT * CT * OWN, 9 << 20),
        name="cell_product",
    )(blocks, counts, before, low, after, tiles)


TURN_STEP = 8


def turn_kernel(tiles_ref, out_ref):
    low = lax.axis_index("core") == 0
    for i in range(TURN_STEP):
        for k in range(SLOTS):
            t = tiles_ref[i, k].astype(jnp.float32)
            top, bottom = t[:OWN], t[OWN:]
            mine = jnp.where(low, top, bottom)
            other = jnp.where(low, bottom, top)
            turned = jnp.concatenate([mine, other], axis=0).T
            kept = jnp.where(low, turned[:OWN], turned[OWN:])
            out_ref[i, :, k * GT : (k + 1) * GT] = kept.astype(jnp.bfloat16)


def turn_tiles(gene_tiles):
    return pl.pallas_call(
        turn_kernel,
        grid=(GB // TURN_STEP,),
        out_shape=jax.ShapeDtypeStruct((GB, OWN, SLOTS * GT), jnp.bfloat16),
        in_specs=[pl.BlockSpec((TURN_STEP, SLOTS, GT, GT), lambda s: (s, 0, 0, 0))],
        out_specs=pl.BlockSpec((TURN_STEP, OWN, SLOTS * GT), lambda s: (s, 0, 0)),
        compiler_params=params(8),
        cost_estimate=cost(1 << 24, 5 << 20),
        name="turn_tiles",
    )(gene_tiles)


def gene_block(blocks_ref, turned_ref, mine_ref, other_ref, a):
    parts = []
    for k in range(SLOTS):
        at = blocks_ref[k, a]
        parts += [mine_ref[at], other_ref[at]]
    return jnp.dot(turned_ref[a], jnp.concatenate(parts, axis=0), preferred_element_type=jnp.float32)


def gene_kernel(blocks_ref, turned_ref, mine_ref, other_ref, cell_ref, d_ref, low_ref, rest_ref):
    for a in range(GB):
        gene = gene_block(blocks_ref, turned_ref, mine_ref, other_ref, a)
        d = soft(cell_ref[a].astype(jnp.float32) + gene)
        sent = d.astype(jnp.bfloat16)
        d_ref[a] = sent
        rest_ref[a] = d - sent.astype(jnp.float32)
        low_ref[a] = (mine_ref[a].astype(jnp.float32) - d).astype(jnp.bfloat16)


def first_gene_step(blocks, turned, mine, other, cell):
    return pl.pallas_call(
        gene_kernel,
        out_shape=[
            jax.ShapeDtypeStruct(CHUNKED, jnp.bfloat16),
            jax.ShapeDtypeStruct(CHUNKED, jnp.bfloat16),
            jax.ShapeDtypeStruct(CHUNKED, jnp.float32),
        ],
        in_specs=[SMEM, VMEM, VMEM, VMEM, VMEM],
        out_specs=[VMEM, VMEM, VMEM],
        compiler_params=params(16),
        cost_estimate=cost(2 * GB * OWN * SLOTS * GT * CHUNK, 5 << 20),
        name="first_gene_step",
    )(blocks, turned, mine, other, cell)


def second_kernel(blocks_ref, turned_ref, mine_ref, other_ref, rest_ref, out_ref):
    for a in range(GB):
        gene = gene_block(blocks_ref, turned_ref, mine_ref, other_ref, a)
        out_ref[a] = (gene + rest_ref[a]).astype(jnp.bfloat16)


def second_gene_step(blocks, turned, mine, other, rest):
    return pl.pallas_call(
        second_kernel,
        out_shape=jax.ShapeDtypeStruct(CHUNKED, jnp.bfloat16),
        in_specs=[SMEM, VMEM, VMEM, VMEM, VMEM],
        out_specs=VMEM,
        compiler_params=params(16),
        cost_estimate=cost(2 * GB * OWN * SLOTS * GT * CHUNK, 5 << 20),
        name="second_gene_step",
    )(blocks, turned, mine, other, rest)


def last_kernel(x_ref, d_ref, gene_ref, cell_ref, out_ref):
    for j in range(CHIPS):
        v = cell_ref[j] + (d_ref[j].astype(jnp.float32) + gene_ref[j].astype(jnp.float32))
        at = slice(j * CHUNK, (j + 1) * CHUNK)
        out_ref[:, at] = x_ref[:, at] - soft(v)


def last_step(x, d, gene, cell):
    return pl.pallas_call(
        last_kernel,
        out_shape=jax.ShapeDtypeStruct(x.shape, jnp.float32),
        in_specs=[VMEM] * 4,
        out_specs=VMEM,
        compiler_params=params(12),
        cost_estimate=cost(1 << 20, 4 << 20),
        name="last_step",
    )(x, d, gene, cell)


def exchange(chunks):
    return lax.all_to_all(chunks, "chip", split_axis=0, concat_axis=0, tiled=True)


def swap_cores(chunks):
    return lax.ppermute(chunks, "core", [(0, 1), (1, 0)])


def halo(low):
    n = lax.axis_size("slab")
    before = lax.ppermute(low[CHIPS - 2 * BEFORE :], "slab", [(i, (i + 1) % n) for i in range(n)])
    after = lax.ppermute(low[: 2 * AFTER], "slab", [((i + 1) % n, i) for i in range(n)])
    return before, after


def local(expression, cell_tiles, cell_blocks, cell_counts, gene_tiles, gene_blocks):
    x = expression.T
    cell_at, gene_at = cell_blocks.T, gene_blocks.T
    low = cast_chunks(x)
    mine = exchange(low)
    before, after = halo(low)
    cell = exchange(cell_product(cell_at, cell_counts, before, low, after, cell_tiles, jnp.bfloat16))
    turned = turn_tiles(gene_tiles)
    d, low_rows, rest = first_gene_step(gene_at, turned, mine, swap_cores(mine), cell)
    d_back = exchange(d)
    gene_back = exchange(second_gene_step(gene_at, turned, low_rows, swap_cores(low_rows), rest))
    low = step_chunks(x, d_back)
    before, after = halo(low)
    cell = cell_product(cell_at, cell_counts, before, low, after, cell_tiles, jnp.float32)
    return last_step(x, d_back, gene_back, cell).T


def solution(mesh):
    slabs, inner = mesh.devices.shape
    wide = Mesh(mesh.devices.reshape(slabs, inner // 2, 2), ("slab", "chip", "core"))
    in_specs = (
        P("slab", ("chip", "core")),
        P("slab", None, None, None),
        P("slab", None),
        P("slab"),
        P(),
        P(),
    )
    out_specs = P("slab", ("chip", "core"))
    return jax.shard_map(local, mesh=wide, in_specs=in_specs, out_specs=out_specs, check_vma=False)
```

time: 484 us -> 103 us (0.21); the launches traced: 475 us -> 102 us
  local copies, waits for them, and re-layouts: 170 us -> 17.3 us
  other arithmetic: 103 us -> 0 us
  blocking collectives: 99 us -> 0 us
  waiting for transfers between devices: 54.6 us -> 35.2 us
  matrix products: 16.9 us -> 0 us
  Pallas kernels: 0 us -> 13.4 us
    all_to_all x3 -> x0, blocking collectives: 99 us -> none  [the longest x1 40.1 us: local(): lax.all_to_all(expression.reshape(parts_inner, per_device, local_genes),...]
    unnamed x3 -> x0, other arithmetic: 69.6 us -> none
    all_to_all x10 -> x0, local copies, waits for them, and re-layouts: 36.8 us -> none  [the longest x6 24.1 us: local(): lax.all_to_all(lowp.reshape(1, per_device, GENES), 'inner', split_axis=2,...]
    unnamed x22 -> x32, local copies, waits for them, and re-layouts: 49.2 us -> 15.7 us
    reshape x13 -> x0, local copies, waits for them, and re-layouts: 32.6 us -> none  [the longest x3 9.55 us: local(): cellterm = cellterm.reshape(per_device, GENES)]
    all_to_all x3 -> x4, waiting for transfers between devices: 54.6 us -> 24.8 us  [exchange(): lax.all_to_all(chunks, 'chip', split_axis=0, concat_axis=0, tiled=True)]
    all_to_all x4 -> x0, other arithmetic: 21.3 us -> none  [the longest x2 10.7 us: local(): lax.all_to_all(cell_group.reshape(parts_inner, per_device, local_genes),...]
    dot_general x4 -> x0, matrix products: 16.9 us -> none  [the longest x2 10.6 us: cell_product(): jnp.einsum('bkij,bkjg->big', cell_tiles, gathered, preferred_element_type...]
  transfers between devices with their start and end apart: 7 -> 10, of which waited for: 3 -> 6; matrix products, arithmetic and copies ran while one was open for 7% -> 2% of each run, Pallas kernels for 0% -> 10%
where the time goes in v1:
time: 103 us; the launch traced here: 102 us
  starting transfers between devices  36.2 us (35%)
  waiting for transfers between devices  35.2 us (34%)
  local copies, waits for them, and re-layouts  17.3 us (17%)
  Pallas kernels  13.4 us (13%)
    all_to_all x4, starting transfers between devices, exchange(): lax.all_to_all(chunks, 'chip', split_axis=0, concat_axis=0, tiled=True)  30.9 us
    all_to_all x4, waiting for transfers between devices, exchange(): lax.all_to_all(chunks, 'chip', split_axis=0, concat_axis=0, tiled=True)  24.8 us
    unnamed x32, local copies, waits for them, and re-layouts  15.7 us
    ppermute x2, waiting for transfers between devices, halo(): lax.ppermute(low[CHIPS - 2 * BEFORE:], 'slab', [(i, (i + 1) % n) for i in...  8.32 us
    pallas_call x2, Pallas kernels, cell_product(): pl.pallas_call(cell_kernel, grid=(BLOCKS // CELL_STEP,), out_shape=jax.Sh...  7.32 us
    ppermute x2, starting transfers between devices, halo(): lax.ppermute(low[:2 * AFTER], 'slab', [((i + 1) % n, i) for i in range(n)])  3.1 us
    ppermute x2, waiting for transfers between devices, swap_cores(): return lax.ppermute(chunks, 'core', [(0, 1), (1, 0)])  2.11 us
  transfers between devices with their start and end apart: 10, of which 6 were waited for; matrix products, arithmetic and copies ran while one was open for 2% of the time, Pallas kernels for 10%

profile of v1, /device:TPU:32, one launch (start us, length us, event | category | flops | bytes accessed | tf_op | source)
XLA Modules:
  0.0 102.3 jit_solution(18139752148586149681)
XLA Ops:
  0.0 1.2 %copy-done.2 = f32[4096,64]{0,1:T(8,128)S(1)} copy-done((f32[4096,64]{0,1:T(8,128)S(1)}, f32[4096,64]{0,1:T(8,128)}, u32[]{:S(2)}) %copy-start.2) | copy-done | bytes 1048600
  1.2 0.8 cast_chunks.1.low_ref
  2.1 11.2 %all-to-all-start = ((bf16[32,64,128]{2,1,0:T(8,128)(2,1)}), bf16[32,64,128]{2,1,0:T(8,128)(2,1)S(1)}, u32[]{:S(2)}, u32[]{:S(2)}) async-start(bf16[32,64,128]{2,1,0:T(8,128)(2,1)} %cast_chunks.1.low_ref), calls=%async_computation | async-start | bytes 1048576 | tf_op jit(solution)/shard_map/all_to_all | solution.py:221
  13.3 0.9 slice.17
  14.1 3.0 %collective-permute-start.2 = (bf16[4,64,128]{2,1,0:T(8,128)(2,1)S(1)}, bf16[4,64,128]{2,1,0:T(8,128)(2,1)S(1)}, u32[]{:S(2)}, u32[]{:S(2)}) collective-permute-start(bf16[4,64,128]{2,1,0:T(8,128)(2,1)S(1)} %slice.17), channel_id=1, source_target_pairs={{64,0},{128,64},{192,128},{0,192},{65,1},{129,65},{193,129},{1,193... | collective-permute-start | bytes 196616 | tf_op jit(solution)/shard_map/ppermute | solution.py:231
  17.1 0.8 slice.16
  17.9 0.0 collective-permute-start.1
  17.9 5.1 %collective-permute-done.1.before_ref = bf16[2,64,128]{2,1,0:T(8,128)(2,1)S(1)} collective-permute-done((bf16[2,64,128]{2,1,0:T(8,128)(2,1)S(1)}, bf16[2,64,128]{2,1,0:T(8,128)(2,1)S(1)}, u32[]{:S(2)}, u32[]{:S(2)}) %collective-permute-start.1) | collective-permute-done | bytes 32800 | tf_op jit(solution)/shard_map/ppermute | solution.py:230
  23.0 0.0 collective-permute-done.2.after_ref
  23.0 2.8 %copy-done = bf16[16,3,256,256]{3,2,1,0:T(8,128)(2,1)S(1)} copy-done((bf16[16,3,256,256]{3,2,1,0:T(8,128)(2,1)S(1)}, bf16[16,3,256,256]{3,2,1,0:T(8,128)(2,1)}, u32[]{:S(2)}) %copy-start) | copy-done | bytes 6291480
  25.8 0.7 copy-done.11
  26.5 0.7 copy-done.14
  27.2 4.2 %cell_product.2 = bf16[32,64,128]{2,1,0:T(8,128)(2,1)} custom-call(s32[3,16]{1,0:T(4,128)S(1)} %bitcast.7, s32[16]{0:T(128)S(1)} %copy-done.14, bf16[2,64,128]{2,1,0:T(8,128)(2,1)S(1)} %collective-permute-done.1.before_ref, bf16[32,64,128]{2,1,0:T(8,128)(2,1)} %cast_chunks.1.low_ref, bf16[4,64,128]{2,1,0:T(8,128)(2,1)S(1)} %collective-permute-done.2.after_ref, ...), custom_call_target="tpu_custom_call" | custom-call | flops 402653184 | bytes 9437184 | tf_op jit(solution)/shard_map/cell_product/pallas_call | solution.py:100
  31.4 0.0 all-to-all-done.mine_ref
  31.4 9.9 %all-to-all-start.1 = ((bf16[32,64,128]{2,1,0:T(8,128)(2,1)}), bf16[32,64,128]{2,1,0:T(8,128)(2,1)S(1)}, u32[]{:S(2)}, u32[]{:S(2)}) async-start(bf16[32,64,128]{2,1,0:T(8,128)(2,1)} %cell_product.2), calls=%async_computation.1 | async-start | bytes 1048576 | tf_op jit(solution)/shard_map/all_to_all | solution.py:221
  41.3 0.1 collective-permute-start
  41.4 0.0 copy-start.4
  41.5 1.9 %copy-done.4 = bf16[32,3,128,128]{3,2,1,0:T(8,128)(2,1)S(1)} copy-done((bf16[32,3,128,128]{3,2,1,0:T(8,128)(2,1)S(1)}, bf16[32,3,128,128]{3,2,1,0:T(8,128)(2,1)}, u32[]{:S(2)}) %copy-start.4) | copy-done | bytes 3145752
  43.3 1.4 %turn_tiles.1.turned_ref = bf16[32,64,384]{2,1,0:T(8,128)(2,1)S(1)} custom-call(bf16[32,3,128,128]{3,2,1,0:T(8,128)(2,1)S(1)} %copy-done.4), custom_call_target="tpu_custom_call" | custom-call | flops 16777216 | bytes 5242880 | tf_op jit(solution)/shard_map/turn_tiles/pallas_call | solution.py:137
  44.7 12.5 %all-to-all-done.1.cell_ref = bf16[32,64,128]{2,1,0:T(8,128)(2,1)S(1)} async-done(((bf16[32,64,128]{2,1,0:T(8,128)(2,1)}), bf16[32,64,128]{2,1,0:T(8,128)(2,1)S(1)}, u32[]{:S(2)}, u32[]{:S(2)}) %all-to-all-start.1) | async-done | bytes 524320 | tf_op jit(solution)/shard_map/all_to_all | solution.py:221
  57.3 0.0 collective-permute-done.other_ref
  57.3 0.0 copy-done.13
  57.3 1.3 %first_gene_step.1 = (bf16[32,64,128]{2,1,0:T(8,128)(2,1)S(1)}, bf16[32,64,128]{2,1,0:T(8,128)(2,1)S(1)}, f32[32,64,128]{2,1,0:T(8,128)S(1)}) custom-call(s32[3,32]{1,0:T(4,128)S(1)} %bitcast.9, bf16[32,64,384]{2,1,0:T(8,128)(2,1)S(1)} %turn_tiles.1.turned_ref, bf16[32,64,128]{2,1,0:T(8,128)(2,1)S(1)} %all-to-all-done.mine_ref, ...), custom_call_target="tpu_custom_call" | custom-call | flops 201326592 | bytes 5242880 | tf_op jit(solution)/shard_map/first_gene_step/pallas_call | solution.py:168
  58.6 0.0 copy-start.6
  58.6 1.0 copy-done.6
  59.6 0.8 copy-done.8
  60.4 0.8 copy-done.9
  61.2 5.0 %all-to-all-start.2 = ((bf16[32,64,128]{2,1,0:T(8,128)(2,1)}), bf16[32,64,128]{2,1,0:T(8,128)(2,1)S(1)}, u32[]{:S(2)}, u32[]{:S(2)}) async-start(bf16[32,64,128]{2,1,0:T(8,128)(2,1)} %copy-done.8), calls=%async_computation.2 | async-start | bytes 1048576 | tf_op jit(solution)/shard_map/all_to_all | solution.py:221
  66.2 0.1 collective-permute-start.3
  66.3 2.1 %collective-permute-done.3.other_ref = bf16[32,64,128]{2,1,0:T(8,128)(2,1)S(1)} collective-permute-done((bf16[32,64,128]{2,1,0:T(8,128)(2,1)}, bf16[32,64,128]{2,1,0:T(8,128)(2,1)S(1)}, u32[]{:S(2)}, u32[]{:S(2)}) %collective-permute-start.3) | collective-permute-done | bytes 524320 | tf_op jit(solution)/shard_map/ppermute | solution.py:225
  68.4 1.2 %copy-done.7 = f32[32,64,128]{2,1,0:T(8,128)S(1)} copy-done((f32[32,64,128]{2,1,0:T(8,128)S(1)}, f32[32,64,128]{2,1,0:T(8,128)}, u32[]{:S(2)}) %copy-start.7) | copy-done | bytes 1048600
  69.6 1.0 %copy-done.10 = bf16[32,64,128]{2,1,0:T(8,128)(2,1)S(1)} copy-done((bf16[32,64,128]{2,1,0:T(8,128)(2,1)S(1)}, bf16[32,64,128]{2,1,0:T(8,128)(2,1)}, u32[]{:S(2)}) %copy-start.10) | copy-done | bytes 524312
  70.7 1.3 %second_gene_step.1 = bf16[32,64,128]{2,1,0:T(8,128)(2,1)S(1)} custom-call(s32[3,32]{1,0:T(4,128)S(1)} %bitcast.10, bf16[32,64,384]{2,1,0:T(8,128)(2,1)S(1)} %turn_tiles.1.turned_ref, bf16[32,64,128]{2,1,0:T(8,128)(2,1)S(1)} %copy-done.10, bf16[32,64,128]{2,1,0:T(8,128)(2,1)S(1)} %collective-permute-done.3.other_ref, f32[32,64,128]{2,1,0:T(8,128)S(1)} %copy-done.7), custom_call_target="tpu_custom_call" | custom-call | flops 201326592 | bytes 5242880 | tf_op jit(solution)/shard_map/second_gene_step/pallas_call | solution.py:190
  72.0 0.0 copy-start.5
  72.0 0.8 copy-done.5
  72.8 8.7 %all-to-all-done.2.d_ref = bf16[32,64,128]{2,1,0:T(8,128)(2,1)S(1)} async-done(((bf16[32,64,128]{2,1,0:T(8,128)(2,1)}), bf16[32,64,128]{2,1,0:T(8,128)(2,1)S(1)}, u32[]{:S(2)}, u32[]{:S(2)}) %all-to-all-start.2) | async-done | bytes 524320 | tf_op jit(solution)/shard_map/all_to_all | solution.py:221
  81.5 4.8 %all-to-all-start.3 = ((bf16[32,64,128]{2,1,0:T(8,128)(2,1)}), bf16[32,64,128]{2,1,0:T(8,128)(2,1)S(1)}, u32[]{:S(2)}, u32[]{:S(2)}) async-start(bf16[32,64,128]{2,1,0:T(8,128)(2,1)} %copy-done.5), calls=%async_computation.3 | async-start | bytes 1048576 | tf_op jit(solution)/shard_map/all_to_all | solution.py:221
  86.3 0.1 step_chunks.1.low_ref
  86.4 0.1 collective-permute-start.5
  86.5 2.0 %collective-permute-start.4 = (bf16[2,64,128]{2,1,0:T(8,128)(2,1)S(1)}, bf16[2,64,128]{2,1,0:T(8,128)(2,1)S(1)}, u32[]{:S(2)}, u32[]{:S(2)}) collective-permute-start(bf16[2,64,128]{2,1,0:T(8,128)(2,1)S(1)} %slice.18), channel_id=1, source_target_pairs={{0,64},{64,128},{128,192},{192,0},{1,65},{65,129},{129,193},{193,1... | collective-permute-start | bytes 98312 | tf_op jit(solution)/shard_map/ppermute | solution.py:230
  88.5 3.2 %collective-permute-done.4.before_ref = bf16[2,64,128]{2,1,0:T(8,128)(2,1)S(1)} collective-permute-done((bf16[2,64,128]{2,1,0:T(8,128)(2,1)S(1)}, bf16[2,64,128]{2,1,0:T(8,128)(2,1)S(1)}, u32[]{:S(2)}, u32[]{:S(2)}) %collective-permute-start.4) | collective-permute-done | bytes 32800 | tf_op jit(solution)/shard_map/ppermute | solution.py:230
  91.7 0.0 collective-permute-done.5.after_ref
  91.7 0.0 copy-done.12
  91.7 0.0 copy-start.1
  91.8 2.8 %copy-done.1 = bf16[16,3,256,256]{3,2,1,0:T(8,128)(2,1)S(1)} copy-done((bf16[16,3,256,256]{3,2,1,0:T(8,128)(2,1)S(1)}, bf16[16,3,256,256]{3,2,1,0:T(8,128)(2,1)}, u32[]{:S(2)}) %copy-start.1) | copy-done | bytes 6291480
  94.5 3.1 %cell_product.3.cell_ref = f32[32,64,128]{2,1,0:T(8,128)S(1)} custom-call(s32[3,16]{1,0:T(4,128)S(1)} %bitcast.8, s32[16]{0:T(128)S(1)} %copy-done.15, bf16[2,64,128]{2,1,0:T(8,128)(2,1)S(1)} %collective-permute-done.4.before_ref, bf16[32,64,128]{2,1,0:T(8,128)(2,1)S(1)} %step_chunks.1.low_ref, bf16[4,64,128]{2,1,0:T(8,128)(2,1)S(1)} %collective-permute-done.5.after_ref, ...), custom_call_target="tpu_custom_call" | custom-call | flops 402653184 | bytes 9437184 | tf_op jit(solution)/shard_map/cell_product/pallas_call | solution.py:100
  97.6 3.5 %all-to-all-done.3.gene_ref = bf16[32,64,128]{2,1,0:T(8,128)(2,1)S(1)} async-done(((bf16[32,64,128]{2,1,0:T(8,128)(2,1)}), bf16[32,64,128]{2,1,0:T(8,128)(2,1)S(1)}, u32[]{:S(2)}, u32[]{:S(2)}) %all-to-all-start.3) | async-done | bytes 524320 | tf_op jit(solution)/shard_map/all_to_all | solution.py:221
  101.1 1.2 %last_step.1 = f32[64,4096]{1,0:T(8,128)} custom-call(f32[64,4096]{1,0:T(8,128)S(1)} %bitcast.6, bf16[32,64,128]{2,1,0:T(8,128)(2,1)S(1)} %all-to-all-done.2.d_ref, bf16[32,64,128]{2,1,0:T(8,128)(2,1)S(1)} %all-to-all-done.3.gene_ref, f32[32,64,128]{2,1,0:T(8,128)S(1)} %cell_product.3.cell_ref), custom_call_target="tpu_custom_call" | custom-call | flops 1048576 | bytes 4194304 | tf_op jit(solution)/shard_map/last_step/pallas_call | solution.py:209
  (16 shorter events, 0.0 us)
Async XLA Ops:
  0.0 1.2 %copy-start.2 = (f32[4096,64]{0,1:T(8,128)S(1)}, f32[4096,64]{0,1:T(8,128)}, u32[]{:S(2)}) copy-start(f32[4096,64]{0,1:T(8,128)} %param.6) | copy-start | bytes 3145732
  2.1 29.3 %all-to-all-start = ((bf16[32,64,128]{2,1,0:T(8,128)(2,1)}), bf16[32,64,128]{2,1,0:T(8,128)(2,1)S(1)}, u32[]{:S(2)}, u32[]{:S(2)}) async-start(bf16[32,64,128]{2,1,0:T(8,128)(2,1)} %cast_chunks.1.low_ref), calls=%async_computation | async-start | bytes 1048576 | tf_op jit(solution)/shard_map/all_to_all | solution.py:221
  14.1 8.9 %collective-permute-start.2 = (bf16[4,64,128]{2,1,0:T(8,128)(2,1)S(1)}, bf16[4,64,128]{2,1,0:T(8,128)(2,1)S(1)}, u32[]{:S(2)}, u32[]{:S(2)}) collective-permute-start(bf16[4,64,128]{2,1,0:T(8,128)(2,1)S(1)} %slice.17), channel_id=1, source_target_pairs={{64,0},{128,64},{192,128},{0,192},{65,1},{129,65},{193,129},{1,193... | collective-permute-start | bytes 196616 | tf_op jit(solution)/shard_map/ppermute | solution.py:231
  17.9 5.1 %collective-permute-start.1 = (bf16[2,64,128]{2,1,0:T(8,128)(2,1)S(1)}, bf16[2,64,128]{2,1,0:T(8,128)(2,1)S(1)}, u32[]{:S(2)}, u32[]{:S(2)}) collective-permute-start(bf16[2,64,128]{2,1,0:T(8,128)(2,1)S(1)} %slice.16), channel_id=1, source_target_pairs={{0,64},{64,128},{128,192},{192,0},{1,65},{65,129},{129,193},{193,1... | collective-permute-start | bytes 98312 | tf_op jit(solution)/shard_map/ppermute | solution.py:230
  23.0 2.8 %copy-start = (bf16[16,3,256,256]{3,2,1,0:T(8,128)(2,1)S(1)}, bf16[16,3,256,256]{3,2,1,0:T(8,128)(2,1)}, u32[]{:S(2)}) copy-start(bf16[16,3,256,256]{3,2,1,0:T(8,128)(2,1)} %tiles_ref.5) | copy-start | bytes 18874372
  25.8 0.7 copy-start.11
  26.5 0.7 copy-start.14
  31.4 25.9 %copy-start.13 = (s32[32,3]{0,1:T(4,128)S(1)}, s32[32,3]{0,1:T(4,128)}, u32[]{:S(2)}) copy-start(s32[32,3]{0,1:T(4,128)} %param.11) | copy-start | bytes 1156
  31.4 25.9 %all-to-all-start.1 = ((bf16[32,64,128]{2,1,0:T(8,128)(2,1)}), bf16[32,64,128]{2,1,0:T(8,128)(2,1)S(1)}, u32[]{:S(2)}, u32[]{:S(2)}) async-start(bf16[32,64,128]{2,1,0:T(8,128)(2,1)} %cell_product.2), calls=%async_computation.1 | async-start | bytes 1048576 | tf_op jit(solution)/shard_map/all_to_all | solution.py:221
  41.3 15.9 %collective-permute-start = (bf16[32,64,128]{2,1,0:T(8,128)(2,1)S(1)}, bf16[32,64,128]{2,1,0:T(8,128)(2,1)S(1)}, u32[]{:S(2)}, u32[]{:S(2)}) collective-permute-start(bf16[32,64,128]{2,1,0:T(8,128)(2,1)S(1)} %all-to-all-done.mine_ref), channel_id=1, source_target_pairs={{0,1},{1,0},{2,3},{3,2},{4,5},{5,4},{6,7},{7,6},{8,9},{9,8},{10,11... | collective-permute-start | bytes 1572872 | tf_op jit(solution)/shard_map/ppermute | solution.py:225
  41.4 1.9 %copy-start.4 = (bf16[32,3,128,128]{3,2,1,0:T(8,128)(2,1)S(1)}, bf16[32,3,128,128]{3,2,1,0:T(8,128)(2,1)}, u32[]{:S(2)}) copy-start(bf16[32,3,128,128]{3,2,1,0:T(8,128)(2,1)} %tiles_ref.3) | copy-start | bytes 9437188
  58.6 1.0 copy-start.6
  59.6 0.8 copy-start.8
  60.4 0.8 copy-start.9
  61.2 25.1 %copy-start.3 = (f32[4096,64]{0,1:T(8,128)S(1)}, f32[4096,64]{0,1:T(8,128)}, u32[]{:S(2)}) copy-start(f32[4096,64]{0,1:T(8,128)} %param.6) | copy-start | bytes 3145732
  61.2 20.3 %all-to-all-start.2 = ((bf16[32,64,128]{2,1,0:T(8,128)(2,1)}), bf16[32,64,128]{2,1,0:T(8,128)(2,1)S(1)}, u32[]{:S(2)}, u32[]{:S(2)}) async-start(bf16[32,64,128]{2,1,0:T(8,128)(2,1)} %copy-done.8), calls=%async_computation.2 | async-start | bytes 1048576 | tf_op jit(solution)/shard_map/all_to_all | solution.py:221
  66.2 2.2 %collective-permute-start.3 = (bf16[32,64,128]{2,1,0:T(8,128)(2,1)}, bf16[32,64,128]{2,1,0:T(8,128)(2,1)S(1)}, u32[]{:S(2)}, u32[]{:S(2)}) collective-permute-start(bf16[32,64,128]{2,1,0:T(8,128)(2,1)} %copy-done.9), channel_id=1, source_target_pairs={{0,1},{1,0},{2,3},{3,2},{4,5},{5,4},{6,7},{7,6},{8,9},{9,8},{10,11... | collective-permute-start | bytes 1572872 | tf_op jit(solution)/shard_map/ppermute | solution.py:225
  68.4 1.2 %copy-start.7 = (f32[32,64,128]{2,1,0:T(8,128)S(1)}, f32[32,64,128]{2,1,0:T(8,128)}, u32[]{:S(2)}) copy-start(f32[32,64,128]{2,1,0:T(8,128)} %copy-done.6) | copy-start | bytes 3145732
  69.6 1.0 %copy-start.10 = (bf16[32,64,128]{2,1,0:T(8,128)(2,1)S(1)}, bf16[32,64,128]{2,1,0:T(8,128)(2,1)}, u32[]{:S(2)}) copy-start(bf16[32,64,128]{2,1,0:T(8,128)(2,1)} %copy-done.9) | copy-start | bytes 1572868
  70.7 21.1 %copy-start.12 = (s32[16,3]{0,1:T(4,128)S(1)}, s32[16,3]{0,1:T(4,128)}, u32[]{:S(2)}) copy-start(s32[16,3]{0,1:T(4,128)} %param.8) | copy-start | bytes 580
  70.7 21.1 %copy-start.15 = (s32[16]{0:T(128)S(1)}, s32[16]{0:T(128)}, u32[]{:S(2)}) copy-start(s32[16]{0:T(128)} %counts_ref.3) | copy-start | bytes 196
  72.0 0.8 copy-start.5
  81.5 19.7 %all-to-all-start.3 = ((bf16[32,64,128]{2,1,0:T(8,128)(2,1)}), bf16[32,64,128]{2,1,0:T(8,128)(2,1)S(1)}, u32[]{:S(2)}, u32[]{:S(2)}) async-start(bf16[32,64,128]{2,1,0:T(8,128)(2,1)} %copy-done.5), calls=%async_computation.3 | async-start | bytes 1048576 | tf_op jit(solution)/shard_map/all_to_all | solution.py:221
  86.4 5.3 %collective-permute-start.5 = (bf16[4,64,128]{2,1,0:T(8,128)(2,1)S(1)}, bf16[4,64,128]{2,1,0:T(8,128)(2,1)S(1)}, u32[]{:S(2)}, u32[]{:S(2)}) collective-permute-start(bf16[4,64,128]{2,1,0:T(8,128)(2,1)S(1)} %slice.19), channel_id=1, source_target_pairs={{64,0},{128,64},{192,128},{0,192},{65,1},{129,65},{193,129},{1,193... | collective-permute-start | bytes 196616 | tf_op jit(solution)/shard_map/ppermute | solution.py:231
  86.5 5.2 %collective-permute-start.4 = (bf16[2,64,128]{2,1,0:T(8,128)(2,1)S(1)}, bf16[2,64,128]{2,1,0:T(8,128)(2,1)S(1)}, u32[]{:S(2)}, u32[]{:S(2)}) collective-permute-start(bf16[2,64,128]{2,1,0:T(8,128)(2,1)S(1)} %slice.18), channel_id=1, source_target_pairs={{0,64},{64,128},{128,192},{192,0},{1,65},{65,129},{129,193},{193,1... | collective-permute-start | bytes 98312 | tf_op jit(solution)/shard_map/ppermute | solution.py:230
  91.7 2.8 %copy-start.1 = (bf16[16,3,256,256]{3,2,1,0:T(8,128)(2,1)S(1)}, bf16[16,3,256,256]{3,2,1,0:T(8,128)(2,1)}, u32[]{:S(2)}) copy-start(bf16[16,3,256,256]{3,2,1,0:T(8,128)(2,1)} %tiles_ref.5) | copy-start | bytes 18874372

commit v2 on v1

v2 whole, which is shorter than its diff:
```python
import jax
import jax.numpy as jnp
from jax import lax
from jax.experimental import pallas as pl
from jax.experimental.pallas import tpu as pltpu
from jax.sharding import Mesh
from jax.sharding import PartitionSpec as P

CHIPS = 32
OWN = 64
CHUNK = 128
BLOCKS = 16
CT = 256
GB = 32
GT = 128
SLOTS = 3
BEFORE, AFTER = 1, 2
HALF = 0.5

VMEM = pl.BlockSpec(memory_space=pltpu.VMEM)
SMEM = pl.BlockSpec(memory_space=pltpu.SMEM)
CHUNKED = (CHIPS, OWN, CHUNK)
DIMS_NT = (((1,), (1,)), ((), ()))


def soft(v):
    return v - jnp.clip(v, -HALF, HALF)


def params(mib):
    return pltpu.CompilerParams(vmem_limit_bytes=mib << 20)


def cost(flops, moved):
    return pl.CostEstimate(flops=flops, bytes_accessed=moved, transcendentals=0)


LOWP_STEP = 4
PART = CHIPS // LOWP_STEP


def low_chunks(values, low_ref, head_ref, tail_ref):
    step = pl.program_id(0)
    low = [values(j).astype(jnp.bfloat16) for j in range(PART)]
    for j in range(PART):
        low_ref[j] = low[j]

    @pl.when(step == 0)
    def _():
        for j in range(2 * AFTER):
            head_ref[j] = low[j]

    @pl.when(step == LOWP_STEP - 1)
    def _():
        for j in range(2 * BEFORE):
            tail_ref[j] = low[PART - 2 * BEFORE + j]


def piece(x_ref, j):
    return x_ref[:, j * CHUNK : (j + 1) * CHUNK]


def cast_kernel(x_ref, low_ref, head_ref, tail_ref):
    low_chunks(lambda j: piece(x_ref, j), low_ref, head_ref, tail_ref)


def move_kernel(x_ref, cell_ref, gene_ref, low_ref, head_ref, tail_ref, d_ref):
    def value(j):
        d = soft(cell_ref[j] + gene_ref[j].astype(jnp.float32))
        d_ref[j] = d
        return piece(x_ref, j) - d

    low_chunks(value, low_ref, head_ref, tail_ref)


X_BLOCK = pl.BlockSpec((OWN, PART * CHUNK), lambda s: (0, s))
PART_BLOCK = pl.BlockSpec((PART, OWN, CHUNK), lambda s: (s, 0, 0))
LOW_SHAPES = [
    jax.ShapeDtypeStruct(CHUNKED, jnp.bfloat16),
    jax.ShapeDtypeStruct((2 * AFTER, OWN, CHUNK), jnp.bfloat16),
    jax.ShapeDtypeStruct((2 * BEFORE, OWN, CHUNK), jnp.bfloat16),
]


def cast_chunks(x):
    return pl.pallas_call(
        cast_kernel,
        grid=(LOWP_STEP,),
        out_shape=LOW_SHAPES,
        in_specs=[X_BLOCK],
        out_specs=[PART_BLOCK, VMEM, VMEM],
        compiler_params=params(8),
        cost_estimate=cost(1 << 18, 3 << 19),
        name="cast_chunks",
    )(x)


def move_chunks(x, cell, gene):
    return pl.pallas_call(
        move_kernel,
        grid=(LOWP_STEP,),
        out_shape=LOW_SHAPES + [jax.ShapeDtypeStruct(CHUNKED, jnp.float32)],
        in_specs=[X_BLOCK, PART_BLOCK, PART_BLOCK],
        out_specs=[PART_BLOCK, VMEM, VMEM, PART_BLOCK],
        compiler_params=params(8),
        cost_estimate=cost(1 << 19, 4 << 20),
        name="move_chunks",
    )(x, cell, gene)


CELL_STEP = 4
CELL_MIB = 48


def cell_blocks_of(refs, tiles_ref, all_ref, put):
    blocks_ref, counts_ref, before_ref, low_ref, after_ref = refs
    step = pl.program_id(0)
    first = lax.axis_index("slab") * BLOCKS - BEFORE

    @pl.when(step == 0)
    def _():
        all_ref[: 2 * BEFORE] = before_ref[...]
        all_ref[2 * BEFORE : 2 * BEFORE + CHIPS] = low_ref[...]
        all_ref[2 * BEFORE + CHIPS :] = after_ref[...]

    for i in range(CELL_STEP):
        b = step * CELL_STEP + i
        total = jnp.zeros((OWN, CT), jnp.float32)
        for k in range(SLOTS):
            at = 2 * (blocks_ref[k, b] - first)
            source = jnp.concatenate([all_ref[at], all_ref[at + 1]], axis=1)
            part = lax.dot_general(source, tiles_ref[i, k], DIMS_NT, preferred_element_type=jnp.float32)
            used = jnp.where(k < counts_ref[b], 1.0, 0.0).astype(jnp.float32)
            total = total + used * part
        put(2 * i, total[:, :CHUNK])
        put(2 * i + 1, total[:, CHUNK:])


def first_cell_kernel(*refs):
    *operands, tiles_ref, out_ref, low_out_ref, all_ref = refs

    def put(j, value):
        out_ref[j] = value
        low_out_ref[j] = value.astype(jnp.bfloat16)

    cell_blocks_of(operands, tiles_ref, all_ref, put)


def second_cell_kernel(*refs):
    *operands, tiles_ref, d_ref, out_ref, all_ref = refs

    def put(j, value):
        out_ref[j] = value + d_ref[j]

    cell_blocks_of(operands, tiles_ref, all_ref, put)


CELL_BLOCK = pl.BlockSpec((2 * CELL_STEP, OWN, CHUNK), lambda s: (s, 0, 0))


def cell_product(kernel, types, operands, tiles, *more):
    return pl.pallas_call(
        kernel,
        grid=(BLOCKS // CELL_STEP,),
        out_shape=[jax.ShapeDtypeStruct(CHUNKED, dtype) for dtype in types],
        in_specs=[
            SMEM,
            SMEM,
            VMEM,
            VMEM,
            VMEM,
            pl.BlockSpec((CELL_STEP, SLOTS, CT, CT), lambda s: (s, 0, 0, 0)),
        ]
        + [CELL_BLOCK] * len(more),
        out_specs=[CELL_BLOCK] * len(types),
        scratch_shapes=[pltpu.VMEM((CHIPS + 2 * (BEFORE + AFTER), OWN, CHUNK), jnp.bfloat16)],
        compiler_params=params(CELL_MIB),
        cost_estimate=cost(2 * BLOCKS * SLOTS * CT * CT * OWN, 9 << 20),
        name="cell_product",
    )(*operands, tiles, *more)


TURN_STEP = 8


def turn_kernel(tiles_ref, out_ref):
    low = lax.axis_index("core") == 0
    for i in range(TURN_STEP):
        for k in range(SLOTS):
            t = tiles_ref[i, k].astype(jnp.float32)
            top, bottom = t[:OWN], t[OWN:]
            mine = jnp.where(low, top, bottom)
            other = jnp.where(low, bottom, top)
            turned = jnp.concatenate([mine, other], axis=0).T
            kept = jnp.where(low, turned[:OWN], turned[OWN:])
            out_ref[i, :, k * GT : (k + 1) * GT] = kept.astype(jnp.bfloat16)


def turn_tiles(gene_tiles):
    return pl.pallas_call(
        turn_kernel,
        grid=(GB // TURN_STEP,),
        out_shape=jax.ShapeDtypeStruct((GB, OWN, SLOTS * GT), jnp.bfloat16),
        in_specs=[pl.BlockSpec((TURN_STEP, SLOTS, GT, GT), lambda s: (s, 0, 0, 0))],
        out_specs=pl.BlockSpec((TURN_STEP, OWN, SLOTS * GT), lambda s: (s, 0, 0)),
        compiler_params=params(8),
        cost_estimate=cost(1 << 24, 5 << 20),
        name="turn_tiles",
    )(gene_tiles)


def gene_block(blocks_ref, turned_ref, mine_ref, other_ref, a):
    parts = []
    for k in range(SLOTS):
        at = blocks_ref[k, a]
        parts += [mine_ref[at], other_ref[at]]
    return jnp.dot(turned_ref[a], jnp.concatenate(parts, axis=0), preferred_element_type=jnp.float32)


GENE_STEP = 16
GENE_BLOCK = pl.BlockSpec((GENE_STEP, OWN, CHUNK), lambda s: (s, 0, 0))


def first_gene_kernel(blocks_ref, turned_ref, mine_ref, other_ref, sent_ref, gene_ref):
    for i in range(GENE_STEP):
        a = pl.program_id(0) * GENE_STEP + i
        gene = gene_block(blocks_ref, turned_ref, mine_ref, other_ref, a)
        sent_ref[i] = gene.astype(jnp.bfloat16)
        gene_ref[i] = gene


def first_gene(blocks, turned, mine, other):
    return pl.pallas_call(
        first_gene_kernel,
        grid=(GB // GENE_STEP,),
        out_shape=[jax.ShapeDtypeStruct(CHUNKED, jnp.bfloat16), jax.ShapeDtypeStruct(CHUNKED, jnp.float32)],
        in_specs=[SMEM, VMEM, VMEM, VMEM],
        out_specs=[GENE_BLOCK, GENE_BLOCK],
        compiler_params=params(16),
        cost_estimate=cost(2 * GB * OWN * SLOTS * GT * CHUNK, 5 << 20),
        name="first_gene",
    )(blocks, turned, mine, other)


def rows_kernel(mine_ref, gene_ref, cell_ref, low_ref, rest_ref):
    for i in range(GENE_STEP):
        gene, cell = gene_ref[i], cell_ref[i].astype(jnp.float32)
        d = soft(cell + gene)
        rest_ref[i] = d - soft(cell + gene.astype(jnp.bfloat16).astype(jnp.float32))
        low_ref[i] = (mine_ref[i].astype(jnp.float32) - d).astype(jnp.bfloat16)


def move_rows(mine, gene, cell):
    return pl.pallas_call(
        rows_kernel,
        grid=(GB // GENE_STEP,),
        out_shape=[jax.ShapeDtypeStruct(CHUNKED, jnp.bfloat16), jax.ShapeDtypeStruct(CHUNKED, jnp.float32)],
        in_specs=[GENE_BLOCK] * 3,
        out_specs=[GENE_BLOCK] * 2,
        compiler_params=params(16),
        cost_estimate=cost(1 << 20, 4 << 20),
        name="move_rows",
    )(mine, gene, cell)


def second_gene_kernel(blocks_ref, turned_ref, mine_ref, other_ref, rest_ref, out_ref):
    for i in range(GENE_STEP):
        a = pl.program_id(0) * GENE_STEP + i
        gene = gene_block(blocks_ref, turned_ref, mine_ref, other_ref, a)
        out_ref[i] = (gene + rest_ref[i]).astype(jnp.bfloat16)


def second_gene(blocks, turned, mine, other, rest):
    return pl.pallas_call(
        second_gene_kernel,
        grid=(GB // GENE_STEP,),
        out_shape=jax.ShapeDtypeStruct(CHUNKED, jnp.bfloat16),
        in_specs=[SMEM, VMEM, VMEM, VMEM, GENE_BLOCK],
        out_specs=GENE_BLOCK,
        compiler_params=params(16),
        cost_estimate=cost(2 * GB * OWN * SLOTS * GT * CHUNK, 5 << 20),
        name="second_gene",
    )(blocks, turned, mine, other, rest)


def last_kernel(x_ref, near_ref, gene_ref, out_ref):
    for j in range(PART):
        at = slice(j * CHUNK, (j + 1) * CHUNK)
        out_ref[:, at] = piece(x_ref, j) - soft(near_ref[j] + gene_ref[j].astype(jnp.float32))


def last_step(x, near, gene):
    return pl.pallas_call(
        last_kernel,
        grid=(LOWP_STEP,),
        out_shape=jax.ShapeDtypeStruct(x.shape, jnp.float32),
        in_specs=[X_BLOCK, PART_BLOCK, PART_BLOCK],
        out_specs=X_BLOCK,
        compiler_params=params(12),
        cost_estimate=cost(1 << 20, 4 << 20),
        name="last_step",
    )(x, near, gene)


def exchange(chunks):
    return lax.all_to_all(chunks, "chip", split_axis=0, concat_axis=0, tiled=True)


def swap_cores(chunks):
    return lax.ppermute(chunks, "core", [(0, 1), (1, 0)])


def halo(head, tail):
    n = lax.axis_size("slab")
    before = lax.ppermute(tail, "slab", [(i, (i + 1) % n) for i in range(n)])
    after = lax.ppermute(head, "slab", [((i + 1) % n, i) for i in range(n)])
    return before, after


def local(expression, cell_tiles, cell_blocks, cell_counts, gene_tiles, gene_blocks):
    x = expression.T
    cell_at, gene_at = cell_blocks.T, gene_blocks.T
    low, head, tail = cast_chunks(x)
    mine = exchange(low)
    before, after = halo(head, tail)
    f32, bf16 = jnp.float32, jnp.bfloat16
    operands = (cell_at, cell_counts, before, low, after)
    cell, cell_sent = cell_product(first_cell_kernel, (f32, bf16), operands, cell_tiles)
    cell_rows = exchange(cell_sent)
    turned = turn_tiles(gene_tiles)
    gene_sent, gene_rows = first_gene(gene_at, turned, mine, swap_cores(mine))
    gene = exchange(gene_sent)
    low_rows, rest = move_rows(mine, gene_rows, cell_rows)
    gene_last = exchange(second_gene(gene_at, turned, low_rows, swap_cores(low_rows), rest))
    low, head, tail, d = move_chunks(x, cell, gene)
    before, after = halo(head, tail)
    operands = (cell_at, cell_counts, before, low, after)
    (near,) = cell_product(second_cell_kernel, (f32,), operands, cell_tiles, d)
    return last_step(x, near, gene_last).T


def solution(mesh):
    slabs, inner = mesh.devices.shape
    wide = Mesh(mesh.devices.reshape(slabs, inner // 2, 2), ("slab", "chip", "core"))
    in_specs = (
        P("slab", ("chip", "core")),
        P("slab", None, None, None),
        P("slab", None),
        P("slab"),
        P(),
        P(),
    )
    out_specs = P("slab", ("chip", "core"))
    return jax.shard_map(local, mesh=wide, in_specs=in_specs, out_specs=out_specs, check_vma=False)
```

time: 103 us -> 98.8 us (0.959)
  local copies, waits for them, and re-layouts: 17.3 us -> 10.4 us
  Pallas kernels: 13.4 us -> 18.8 us
  waiting for transfers between devices: 35.2 us -> 33.2 us
  starting transfers between devices: 36.2 us -> 34.8 us
    pallas_call x7 -> x8, Pallas kernels: 12.1 us -> 17.4 us  [the longest x2 10.5 us: cell_product(): pl.pallas_call(kernel, grid=(BLOCKS // CELL_STEP,), out_shape=[jax.ShapeD...]
    unnamed x32 -> x28, local copies, waits for them, and re-layouts: 15.7 us -> 10.4 us
    all_to_all x4, waiting for transfers between devices: 24.8 us -> 22.4 us  [exchange(): lax.all_to_all(chunks, 'chip', split_axis=0, concat_axis=0, tiled=True)]
    slice x4 -> x0, local copies, waits for them, and re-layouts: 1.63 us -> none  [the longest x2 0.87 us: halo(): low[:2 * AFTER]]
    all_to_all x4, starting transfers between devices: 30.9 us -> 29.4 us  [exchange(): lax.all_to_all(chunks, 'chip', split_axis=0, concat_axis=0, tiled=True)]
  transfers between devices with their start and end apart: 10 -> 10, of which waited for: 6 -> 7; matrix products, arithmetic and copies ran while one was open for 2% -> 0% of each run, Pallas kernels for 10% -> 16%
where the time goes in v2:
time: 98.8 us; the launch traced here: 97.4 us
  starting transfers between devices  34.8 us (35%)
  waiting for transfers between devices  33.2 us (34%)
  Pallas kernels  18.8 us (19%)
  local copies, waits for them, and re-layouts  10.4 us (11%)
    all_to_all x4, starting transfers between devices, exchange(): lax.all_to_all(chunks, 'chip', split_axis=0, concat_axis=0, tiled=True)  29.4 us
    all_to_all x4, waiting for transfers between devices, exchange(): lax.all_to_all(chunks, 'chip', split_axis=0, concat_axis=0, tiled=True)  22.4 us
    pallas_call x2, Pallas kernels, cell_product(): pl.pallas_call(kernel, grid=(BLOCKS // CELL_STEP,), out_shape=[jax.ShapeD...  10.5 us
    unnamed x28, local copies, waits for them, and re-layouts  10.4 us
    ppermute x2, waiting for transfers between devices, halo(): before = lax.ppermute(tail, 'slab', [(i, (i + 1) % n) for i in range(n)])  8.86 us
    ppermute x2, starting transfers between devices, halo(): after = lax.ppermute(head, 'slab', [((i + 1) % n, i) for i in range(n)])  3.81 us
  transfers between devices with their start and end apart: 10, of which 7 were waited for; matrix products, arithmetic and copies ran while one was open for 0% of the time, Pallas kernels for 16%

profile of v2, /device:TPU:32, one launch (start us, length us, event | category | flops | bytes accessed | tf_op | source)
XLA Modules:
  0.0 97.4 jit_solution(3059861814499165218)
XLA Ops:
  0.0 1.2 %copy-done = f32[4096,64]{0,1:T(8,128)S(1)} copy-done((f32[4096,64]{0,1:T(8,128)S(1)}, f32[4096,64]{0,1:T(8,128)}, u32[]{:S(2)}) %copy-start) | copy-done | bytes 1048600
  1.2 1.5 %cast_chunks.1 = (bf16[32,64,128]{2,1,0:T(8,128)(2,1)}, bf16[4,64,128]{2,1,0:T(8,128)(2,1)S(1)}, bf16[2,64,128]{2,1,0:T(8,128)(2,1)S(1)}) custom-call(f32[64,4096]{1,0:T(8,128)S(1)} %bitcast.4), custom_call_target="tpu_custom_call" | custom-call | flops 262144 | bytes 1572864 | tf_op jit(solution)/shard_map/cast_chunks/pallas_call | solution.py:86
  2.7 11.2 %all-to-all-start = ((bf16[32,64,128]{2,1,0:T(8,128)(2,1)}), bf16[32,64,128]{2,1,0:T(8,128)(2,1)S(1)}, u32[]{:S(2)}, u32[]{:S(2)}) async-start(bf16[32,64,128]{2,1,0:T(8,128)(2,1)} %get-tuple-element.19.refs_3_), calls=%async_computation | async-start | bytes 1048576 | tf_op jit(solution)/shard_map/all_to_all | solution.py:306
  13.9 3.1 %collective-permute-start.1 = (bf16[4,64,128]{2,1,0:T(8,128)(2,1)S(1)}, bf16[4,64,128]{2,1,0:T(8,128)(2,1)S(1)}, u32[]{:S(2)}, u32[]{:S(2)}) collective-permute-start(bf16[4,64,128]{2,1,0:T(8,128)(2,1)S(1)} %get-tuple-element.20), channel_id=1, source_target_pairs={{64,0},{128,64},{192,128},{0,192},{65,1},{129,65},{193,129},{1,193... | collective-permute-start | bytes 196616 | tf_op jit(solution)/shard_map/ppermute | solution.py:316
  17.0 0.0 collective-permute-start
  17.0 5.1 %collective-permute-done.refs_2_ = bf16[2,64,128]{2,1,0:T(8,128)(2,1)S(1)} collective-permute-done((bf16[2,64,128]{2,1,0:T(8,128)(2,1)S(1)}, bf16[2,64,128]{2,1,0:T(8,128)(2,1)S(1)}, u32[]{:S(2)}, u32[]{:S(2)}) %collective-permute-start) | collective-permute-done | bytes 32800 | tf_op jit(solution)/shard_map/ppermute | solution.py:315
  22.1 0.0 collective-permute-done.1.refs_4_
  22.1 0.7 copy-done.9
  22.8 0.7 copy-done.12
  23.5 5.7 %cell_product.2 = (f32[32,64,128]{2,1,0:T(8,128)S(1)}, bf16[32,64,128]{2,1,0:T(8,128)(2,1)}) custom-call(s32[3,16]{1,0:T(4,128)S(1)} %bitcast.7, s32[16]{0:T(128)S(1)} %copy-done.12, bf16[2,64,128]{2,1,0:T(8,128)(2,1)S(1)} %collective-permute-done.refs_2_, bf16[32,64,128]{2,1,0:T(8,128)(2,1)} %get-tuple-element.19.refs_3_, ...), custom_call_target="tpu_custom_call" | custom-call | flops 402653184 | bytes 9437184 | tf_op jit(solution)/shard_map/cell_product/pallas_call | solution.py:162
  29.1 1.0 copy-done.4
  30.1 1.4 %all-to-all-done.mine_ref = bf16[32,64,128]{2,1,0:T(8,128)(2,1)S(1)} async-done(((bf16[32,64,128]{2,1,0:T(8,128)(2,1)}), bf16[32,64,128]{2,1,0:T(8,128)(2,1)S(1)}, u32[]{:S(2)}, u32[]{:S(2)}) %all-to-all-start) | async-done | bytes 524320 | tf_op jit(solution)/shard_map/all_to_all | solution.py:306
  31.5 8.5 %all-to-all-start.2 = ((bf16[32,64,128]{2,1,0:T(8,128)(2,1)}), bf16[32,64,128]{2,1,0:T(8,128)(2,1)S(1)}, u32[]{:S(2)}, u32[]{:S(2)}) async-start(bf16[32,64,128]{2,1,0:T(8,128)(2,1)} %get-tuple-element.28), calls=%async_computation.2 | async-start | bytes 1048576 | tf_op jit(solution)/shard_map/all_to_all | solution.py:306
  40.0 0.1 collective-permute-start.2
  40.1 0.0 copy-start.2
  40.1 1.9 %copy-done.2 = bf16[32,3,128,128]{3,2,1,0:T(8,128)(2,1)S(1)} copy-done((bf16[32,3,128,128]{3,2,1,0:T(8,128)(2,1)S(1)}, bf16[32,3,128,128]{3,2,1,0:T(8,128)(2,1)}, u32[]{:S(2)}) %copy-start.2) | copy-done | bytes 3145752
  42.0 1.4 %turn_tiles.1.turned_ref = bf16[32,64,384]{2,1,0:T(8,128)(2,1)S(1)} custom-call(bf16[32,3,128,128]{3,2,1,0:T(8,128)(2,1)S(1)} %copy-done.2), custom_call_target="tpu_custom_call" | custom-call | flops 16777216 | bytes 5242880 | tf_op jit(solution)/shard_map/turn_tiles/pallas_call | solution.py:200
  43.4 0.0 collective-permute-done.2.other_ref
  43.4 0.0 copy-done.11
  43.4 1.5 %first_gene.1 = (bf16[32,64,128]{2,1,0:T(8,128)(2,1)S(1)}, f32[32,64,128]{2,1,0:T(8,128)S(1)}) custom-call(s32[3,32]{1,0:T(4,128)S(1)} %bitcast.9, bf16[32,64,384]{2,1,0:T(8,128)(2,1)S(1)} %turn_tiles.1.turned_ref, bf16[32,64,128]{2,1,0:T(8,128)(2,1)S(1)} %all-to-all-done.mine_ref, bf16[32,64,128]{2,1,0:T(8,128)(2,1)S(1)} %collective-permute-done.2.other_ref), custom_call_target="tpu_custom_call" | custom-call | flops 201326592 | bytes 5242880 | tf_op jit(solution)/shard_map/first_gene/pallas_call | solution.py:233
  44.9 0.0 copy-start.6
  44.9 1.0 copy-done.6
  45.9 0.8 copy-done.8
  46.7 9.3 %all-to-all-done.2.cell_ref = bf16[32,64,128]{2,1,0:T(8,128)(2,1)S(1)} async-done(((bf16[32,64,128]{2,1,0:T(8,128)(2,1)}), bf16[32,64,128]{2,1,0:T(8,128)(2,1)S(1)}, u32[]{:S(2)}, u32[]{:S(2)}) %all-to-all-start.2) | async-done | bytes 524320 | tf_op jit(solution)/shard_map/all_to_all | solution.py:306
  56.0 4.8 %all-to-all-start.1 = ((bf16[32,64,128]{2,1,0:T(8,128)(2,1)}), bf16[32,64,128]{2,1,0:T(8,128)(2,1)S(1)}, u32[]{:S(2)}, u32[]{:S(2)}) async-start(bf16[32,64,128]{2,1,0:T(8,128)(2,1)} %copy-done.8), calls=%async_computation.1 | async-start | bytes 1048576 | tf_op jit(solution)/shard_map/all_to_all | solution.py:306
  60.8 0.0 copy-start.7
  60.8 1.2 %copy-done.7 = f32[32,64,128]{2,1,0:T(8,128)S(1)} copy-done((f32[32,64,128]{2,1,0:T(8,128)S(1)}, f32[32,64,128]{2,1,0:T(8,128)}, u32[]{:S(2)}) %copy-start.7) | copy-done | bytes 1048600
  62.0 0.4 move_rows.1
  62.5 0.0 copy-start.1
  62.5 0.1 collective-permute-start.5
  62.6 1.9 %collective-permute-done.5.other_ref = bf16[32,64,128]{2,1,0:T(8,128)(2,1)S(1)} collective-permute-done((bf16[32,64,128]{2,1,0:T(8,128)(2,1)S(1)}, bf16[32,64,128]{2,1,0:T(8,128)(2,1)S(1)}, u32[]{:S(2)}, u32[]{:S(2)}) %collective-permute-start.5) | collective-permute-done | bytes 524320 | tf_op jit(solution)/shard_map/ppermute | solution.py:310
  64.5 1.5 %second_gene.1 = bf16[32,64,128]{2,1,0:T(8,128)(2,1)S(1)} custom-call(s32[3,32]{1,0:T(4,128)S(1)} %bitcast.10, bf16[32,64,384]{2,1,0:T(8,128)(2,1)S(1)} %turn_tiles.1.turned_ref, bf16[32,64,128]{2,1,0:T(8,128)(2,1)S(1)} %get-tuple-element.29.mine_ref, bf16[32,64,128]{2,1,0:T(8,128)(2,1)S(1)} %collective-permute-done.5.other_ref, ...), custom_call_target="tpu_custom_call" | custom-call | flops 201326592 | bytes 5242880 | tf_op jit(solution)/shard_map/second_gene/pallas_call | solution.py:274
  66.0 0.0 copy-start.3
  66.0 0.8 copy-done.3
  66.8 9.3 %all-to-all-done.1.gene_ref = bf16[32,64,128]{2,1,0:T(8,128)(2,1)S(1)} async-done(((bf16[32,64,128]{2,1,0:T(8,128)(2,1)}), bf16[32,64,128]{2,1,0:T(8,128)(2,1)S(1)}, u32[]{:S(2)}, u32[]{:S(2)}) %all-to-all-start.1) | async-done | bytes 524320 | tf_op jit(solution)/shard_map/all_to_all | solution.py:306
  76.1 4.8 %all-to-all-start.3 = ((bf16[32,64,128]{2,1,0:T(8,128)(2,1)}), bf16[32,64,128]{2,1,0:T(8,128)(2,1)S(1)}, u32[]{:S(2)}, u32[]{:S(2)}) async-start(bf16[32,64,128]{2,1,0:T(8,128)(2,1)} %copy-done.3), calls=%async_computation.3 | async-start | bytes 1048576 | tf_op jit(solution)/shard_map/all_to_all | solution.py:306
  80.9 0.0 copy-done.1
  81.0 0.0 copy-start.5
  81.0 1.2 %copy-done.5 = f32[32,64,128]{2,1,0:T(8,128)S(1)} copy-done((f32[32,64,128]{2,1,0:T(8,128)S(1)}, f32[32,64,128]{2,1,0:T(8,128)}, u32[]{:S(2)}) %copy-start.5) | copy-done | bytes 1048600
  82.2 0.4 move_chunks.1
  82.6 0.7 collective-permute-start.4
  83.3 1.4 %collective-permute-start.3 = (bf16[2,64,128]{2,1,0:T(8,128)(2,1)S(1)}, bf16[2,64,128]{2,1,0:T(8,128)(2,1)S(1)}, u32[]{:S(2)}, u32[]{:S(2)}) collective-permute-start(bf16[2,64,128]{2,1,0:T(8,128)(2,1)S(1)} %get-tuple-element.23), channel_id=1, source_target_pairs={{0,64},{64,128},{128,192},{192,0},{1,65},{65,129},{129,193},{193,1... | collective-permute-start | bytes 98312 | tf_op jit(solution)/shard_map/ppermute | solution.py:315
  84.7 3.7 %collective-permute-done.3.refs_2_ = bf16[2,64,128]{2,1,0:T(8,128)(2,1)S(1)} collective-permute-done((bf16[2,64,128]{2,1,0:T(8,128)(2,1)S(1)}, bf16[2,64,128]{2,1,0:T(8,128)(2,1)S(1)}, u32[]{:S(2)}, u32[]{:S(2)}) %collective-permute-start.3) | collective-permute-done | bytes 32800 | tf_op jit(solution)/shard_map/ppermute | solution.py:315
  88.4 0.0 collective-permute-done.4.refs_4_
  88.4 0.0 copy-done.10
  88.4 4.9 %cell_product.3.near_ref = f32[32,64,128]{2,1,0:T(8,128)S(1)} custom-call(s32[3,16]{1,0:T(4,128)S(1)} %bitcast.8, s32[16]{0:T(128)S(1)} %copy-done.13, bf16[2,64,128]{2,1,0:T(8,128)(2,1)S(1)} %collective-permute-done.3.refs_2_, bf16[32,64,128]{2,1,0:T(8,128)(2,1)S(1)} %get-tuple-element.24.refs_3_, bf16[4,64,128]{2,1,0:T(8,128)(2,1)S(1)} %collective-permute-done.4.refs_4_, ...), custom_call_target="tpu_custom_call" | custom-call | flops 402653184 | bytes 9437184 | tf_op jit(solution)/shard_map/cell_product/pallas_call | solution.py:162
  93.3 2.5 %all-to-all-done.3.gene_ref = bf16[32,64,128]{2,1,0:T(8,128)(2,1)S(1)} async-done(((bf16[32,64,128]{2,1,0:T(8,128)(2,1)}), bf16[32,64,128]{2,1,0:T(8,128)(2,1)S(1)}, u32[]{:S(2)}, u32[]{:S(2)}) %all-to-all-start.3) | async-done | bytes 524320 | tf_op jit(solution)/shard_map/all_to_all | solution.py:306
  95.8 1.7 %last_step.1 = f32[64,4096]{1,0:T(8,128)} custom-call(f32[64,4096]{1,0:T(8,128)S(1)} %bitcast.6, f32[32,64,128]{2,1,0:T(8,128)S(1)} %cell_product.3.near_ref, bf16[32,64,128]{2,1,0:T(8,128)(2,1)S(1)} %all-to-all-done.3.gene_ref), custom_call_target="tpu_custom_call" | custom-call | flops 1048576 | bytes 4194304 | tf_op jit(solution)/shard_map/last_step/pallas_call | solution.py:293
  (9 shorter events, 0.0 us)
Async XLA Ops:
  0.0 1.2 %copy-start = (f32[4096,64]{0,1:T(8,128)S(1)}, f32[4096,64]{0,1:T(8,128)}, u32[]{:S(2)}) copy-start(f32[4096,64]{0,1:T(8,128)} %param.6) | copy-start | bytes 3145732
  2.7 28.8 %all-to-all-start = ((bf16[32,64,128]{2,1,0:T(8,128)(2,1)}), bf16[32,64,128]{2,1,0:T(8,128)(2,1)S(1)}, u32[]{:S(2)}, u32[]{:S(2)}) async-start(bf16[32,64,128]{2,1,0:T(8,128)(2,1)} %get-tuple-element.19.refs_3_), calls=%async_computation | async-start | bytes 1048576 | tf_op jit(solution)/shard_map/all_to_all | solution.py:306
  13.9 8.2 %collective-permute-start.1 = (bf16[4,64,128]{2,1,0:T(8,128)(2,1)S(1)}, bf16[4,64,128]{2,1,0:T(8,128)(2,1)S(1)}, u32[]{:S(2)}, u32[]{:S(2)}) collective-permute-start(bf16[4,64,128]{2,1,0:T(8,128)(2,1)S(1)} %get-tuple-element.20), channel_id=1, source_target_pairs={{64,0},{128,64},{192,128},{0,192},{65,1},{129,65},{193,129},{1,193... | collective-permute-start | bytes 196616 | tf_op jit(solution)/shard_map/ppermute | solution.py:316
  17.0 5.1 %collective-permute-start = (bf16[2,64,128]{2,1,0:T(8,128)(2,1)S(1)}, bf16[2,64,128]{2,1,0:T(8,128)(2,1)S(1)}, u32[]{:S(2)}, u32[]{:S(2)}) collective-permute-start(bf16[2,64,128]{2,1,0:T(8,128)(2,1)S(1)} %get-tuple-element.18), channel_id=1, source_target_pairs={{0,64},{64,128},{128,192},{192,0},{1,65},{65,129},{129,193},{193,1... | collective-permute-start | bytes 98312 | tf_op jit(solution)/shard_map/ppermute | solution.py:315
  22.1 0.7 copy-start.9
  22.8 0.7 copy-start.12
  29.1 1.0 copy-start.4
  30.1 13.3 %copy-start.11 = (s32[32,3]{0,1:T(4,128)S(1)}, s32[32,3]{0,1:T(4,128)}, u32[]{:S(2)}) copy-start(s32[32,3]{0,1:T(4,128)} %param.11) | copy-start | bytes 1156
  31.5 24.4 %all-to-all-start.2 = ((bf16[32,64,128]{2,1,0:T(8,128)(2,1)}), bf16[32,64,128]{2,1,0:T(8,128)(2,1)S(1)}, u32[]{:S(2)}, u32[]{:S(2)}) async-start(bf16[32,64,128]{2,1,0:T(8,128)(2,1)} %get-tuple-element.28), calls=%async_computation.2 | async-start | bytes 1048576 | tf_op jit(solution)/shard_map/all_to_all | solution.py:306
  40.0 3.4 %collective-permute-start.2 = (bf16[32,64,128]{2,1,0:T(8,128)(2,1)S(1)}, bf16[32,64,128]{2,1,0:T(8,128)(2,1)S(1)}, u32[]{:S(2)}, u32[]{:S(2)}) collective-permute-start(bf16[32,64,128]{2,1,0:T(8,128)(2,1)S(1)} %all-to-all-done.mine_ref), channel_id=1, source_target_pairs={{0,1},{1,0},{2,3},{3,2},{4,5},{5,4},{6,7},{7,6},{8,9},{9,8},{10,11... | collective-permute-start | bytes 1572872 | tf_op jit(solution)/shard_map/ppermute | solution.py:310
  40.1 1.9 %copy-start.2 = (bf16[32,3,128,128]{3,2,1,0:T(8,128)(2,1)S(1)}, bf16[32,3,128,128]{3,2,1,0:T(8,128)(2,1)}, u32[]{:S(2)}) copy-start(bf16[32,3,128,128]{3,2,1,0:T(8,128)(2,1)} %tiles_ref.1) | copy-start | bytes 9437188
  44.9 1.0 %copy-start.6 = (f32[32,64,128]{2,1,0:T(8,128)}, f32[32,64,128]{2,1,0:T(8,128)S(1)}, u32[]{:S(2)}) copy-start(f32[32,64,128]{2,1,0:T(8,128)S(1)} %get-tuple-element.27.gene_ref) | copy-start | bytes 3145732
  45.9 0.8 copy-start.8
  56.0 20.1 %all-to-all-start.1 = ((bf16[32,64,128]{2,1,0:T(8,128)(2,1)}), bf16[32,64,128]{2,1,0:T(8,128)(2,1)S(1)}, u32[]{:S(2)}, u32[]{:S(2)}) async-start(bf16[32,64,128]{2,1,0:T(8,128)(2,1)} %copy-done.8), calls=%async_computation.1 | async-start | bytes 1048576 | tf_op jit(solution)/shard_map/all_to_all | solution.py:306
  60.8 1.2 %copy-start.7 = (f32[32,64,128]{2,1,0:T(8,128)S(1)}, f32[32,64,128]{2,1,0:T(8,128)}, u32[]{:S(2)}) copy-start(f32[32,64,128]{2,1,0:T(8,128)} %copy-done.6) | copy-start | bytes 3145732
  62.5 18.5 %copy-start.1 = (f32[4096,64]{0,1:T(8,128)S(1)}, f32[4096,64]{0,1:T(8,128)}, u32[]{:S(2)}) copy-start(f32[4096,64]{0,1:T(8,128)} %param.6) | copy-start | bytes 3145732
  62.5 2.0 %collective-permute-start.5 = (bf16[32,64,128]{2,1,0:T(8,128)(2,1)S(1)}, bf16[32,64,128]{2,1,0:T(8,128)(2,1)S(1)}, u32[]{:S(2)}, u32[]{:S(2)}) collective-permute-start(bf16[32,64,128]{2,1,0:T(8,128)(2,1)S(1)} %get-tuple-element.29.mine_ref), channel_id=1, source_target_pairs={{0,1},{1,0},{2,3},{3,2},{4,5},{5,4},{6,7},{7,6},{8,9},{9,8},{10,11... | collective-permute-start | bytes 1572872 | tf_op jit(solution)/shard_map/ppermute | solution.py:310
  64.5 23.9 %copy-start.10 = (s32[16,3]{0,1:T(4,128)S(1)}, s32[16,3]{0,1:T(4,128)}, u32[]{:S(2)}) copy-start(s32[16,3]{0,1:T(4,128)} %param.8) | copy-start | bytes 580
  64.5 23.9 %copy-start.13 = (s32[16]{0:T(128)S(1)}, s32[16]{0:T(128)}, u32[]{:S(2)}) copy-start(s32[16]{0:T(128)} %refs_1_.3) | copy-start | bytes 196
  66.0 0.8 copy-start.3
  76.1 19.7 %all-to-all-start.3 = ((bf16[32,64,128]{2,1,0:T(8,128)(2,1)}), bf16[32,64,128]{2,1,0:T(8,128)(2,1)S(1)}, u32[]{:S(2)}, u32[]{:S(2)}) async-start(bf16[32,64,128]{2,1,0:T(8,128)(2,1)} %copy-done.3), calls=%async_computation.3 | async-start | bytes 1048576 | tf_op jit(solution)/shard_map/all_to_all | solution.py:306
  81.0 1.2 %copy-start.5 = (f32[32,64,128]{2,1,0:T(8,128)S(1)}, f32[32,64,128]{2,1,0:T(8,128)}, u32[]{:S(2)}) copy-start(f32[32,64,128]{2,1,0:T(8,128)} %copy-done.4) | copy-start | bytes 3145732
  82.6 5.8 %collective-permute-start.4 = (bf16[4,64,128]{2,1,0:T(8,128)(2,1)S(1)}, bf16[4,64,128]{2,1,0:T(8,128)(2,1)S(1)}, u32[]{:S(2)}, u32[]{:S(2)}) collective-permute-start(bf16[4,64,128]{2,1,0:T(8,128)(2,1)S(1)} %get-tuple-element.25), channel_id=1, source_target_pairs={{64,0},{128,64},{192,128},{0,192},{65,1},{129,65},{193,129},{1,193... | collective-permute-start | bytes 196616 | tf_op jit(solution)/shard_map/ppermute | solution.py:316
  83.3 5.1 %collective-permute-start.3 = (bf16[2,64,128]{2,1,0:T(8,128)(2,1)S(1)}, bf16[2,64,128]{2,1,0:T(8,128)(2,1)S(1)}, u32[]{:S(2)}, u32[]{:S(2)}) collective-permute-start(bf16[2,64,128]{2,1,0:T(8,128)(2,1)S(1)} %get-tuple-element.23), channel_id=1, source_target_pairs={{0,64},{64,128},{128,192},{192,0},{1,65},{65,129},{129,193},{193,1... | collective-permute-start | bytes 98312 | tf_op jit(solution)/shard_map/ppermute | solution.py:315

commit v3 on v2

--- a/solution.py
+++ b/solution.py
@@ -283,20 +283,28 @@
     )(blocks, turned, mine, other, rest)
 
 
-def last_kernel(x_ref, near_ref, gene_ref, out_ref):
-    for j in range(PART):
-        at = slice(j * CHUNK, (j + 1) * CHUNK)
-        out_ref[:, at] = piece(x_ref, j) - soft(near_ref[j] + gene_ref[j].astype(jnp.float32))
+def last_kernel(x_ref, near_ref, gene_ref, out_ref, ready_ref, sems):
+    copies = []
+    for s in range(LOWP_STEP):
+        at = slice(s * PART * CHUNK, (s + 1) * PART * CHUNK)
+        for j in range(s * PART, (s + 1) * PART):
+            v = near_ref[j] + gene_ref[j].astype(jnp.float32)
+            ready_ref[:, j * CHUNK : (j + 1) * CHUNK] = piece(x_ref, j) - soft(v)
+        copy = pltpu.make_async_copy(ready_ref.at[:, at], out_ref.at[:, at], sems.at[s])
+        copy.start()
+        copies.append(copy)
+    for copy in copies:
+        copy.wait()
 
 
 def last_step(x, near, gene):
     return pl.pallas_call(
         last_kernel,
-        grid=(LOWP_STEP,),
         out_shape=jax.ShapeDtypeStruct(x.shape, jnp.float32),
-        in_specs=[X_BLOCK, PART_BLOCK, PART_BLOCK],
-        out_specs=X_BLOCK,
-        compiler_params=params(12),
+        in_specs=[VMEM] * 3,
+        out_specs=pl.BlockSpec(memory_space=pl.ANY),
+        scratch_shapes=[pltpu.VMEM((OWN, CHIPS * CHUNK), jnp.float32), pltpu.SemaphoreType.DMA((LOWP_STEP,))],
+        compiler_params=params(8),
         cost_estimate=cost(1 << 20, 4 << 20),
         name="last_step",
     )(x, near, gene)

time: 98.8 us -> 98.2 us (level)
  no operation moved by 1% of the time
where the time goes in v3:
time: 98.2 us; the launch traced here: 96.8 us
  starting transfers between devices  34.8 us (35%)
  waiting for transfers between devices  33.2 us (34%)
  Pallas kernels  18.2 us (19%)
  local copies, waits for them, and re-layouts  10.4 us (11%)
    all_to_all x4, starting transfers between devices, exchange(): lax.all_to_all(chunks, 'chip', split_axis=0, concat_axis=0, tiled=True)  29.4 us
    all_to_all x4, waiting for transfers between devices, exchange(): lax.all_to_all(chunks, 'chip', split_axis=0, concat_axis=0, tiled=True)  22.4 us
    pallas_call x2, Pallas kernels, cell_product(): pl.pallas_call(kernel, grid=(BLOCKS // CELL_STEP,), out_shape=[jax.ShapeD...  10.5 us
    unnamed x28, local copies, waits for them, and re-layouts  10.4 us
    ppermute x2, waiting for transfers between devices, halo(): before = lax.ppermute(tail, 'slab', [(i, (i + 1) % n) for i in range(n)])  8.86 us
    ppermute x2, starting transfers between devices, halo(): after = lax.ppermute(head, 'slab', [((i + 1) % n, i) for i in range(n)])  3.81 us
  transfers between devices with their start and end apart: 10, of which 7 were waited for; matrix products, arithmetic and copies ran while one was open for 0% of the time, Pallas kernels for 16%

profile of v3, /device:TPU:32, one launch (start us, length us, event | category | flops | bytes accessed | tf_op | source)
XLA Modules:
  0.0 96.8 jit_solution(17211535899018271126)
XLA Ops:
  0.0 1.2 %copy-done = f32[4096,64]{0,1:T(8,128)S(1)} copy-done((f32[4096,64]{0,1:T(8,128)S(1)}, f32[4096,64]{0,1:T(8,128)}, u32[]{:S(2)}) %copy-start) | copy-done | bytes 1048600
  1.2 1.5 %cast_chunks.1 = (bf16[32,64,128]{2,1,0:T(8,128)(2,1)}, bf16[4,64,128]{2,1,0:T(8,128)(2,1)S(1)}, bf16[2,64,128]{2,1,0:T(8,128)(2,1)S(1)}) custom-call(f32[64,4096]{1,0:T(8,128)S(1)} %bitcast.4), custom_call_target="tpu_custom_call" | custom-call | flops 262144 | bytes 1572864 | tf_op jit(solution)/shard_map/cast_chunks/pallas_call | solution.py:86
  2.7 11.2 %all-to-all-start = ((bf16[32,64,128]{2,1,0:T(8,128)(2,1)}), bf16[32,64,128]{2,1,0:T(8,128)(2,1)S(1)}, u32[]{:S(2)}, u32[]{:S(2)}) async-start(bf16[32,64,128]{2,1,0:T(8,128)(2,1)} %get-tuple-element.19.refs_3_), calls=%async_computation | async-start | bytes 1048576 | tf_op jit(solution)/shard_map/all_to_all | solution.py:314
  13.9 3.1 %collective-permute-start.1 = (bf16[4,64,128]{2,1,0:T(8,128)(2,1)S(1)}, bf16[4,64,128]{2,1,0:T(8,128)(2,1)S(1)}, u32[]{:S(2)}, u32[]{:S(2)}) collective-permute-start(bf16[4,64,128]{2,1,0:T(8,128)(2,1)S(1)} %get-tuple-element.20), channel_id=1, source_target_pairs={{64,0},{128,64},{192,128},{0,192},{65,1},{129,65},{193,129},{1,193... | collective-permute-start | bytes 196616 | tf_op jit(solution)/shard_map/ppermute | solution.py:324
  17.0 0.0 collective-permute-start
  17.0 5.1 %collective-permute-done.refs_2_ = bf16[2,64,128]{2,1,0:T(8,128)(2,1)S(1)} collective-permute-done((bf16[2,64,128]{2,1,0:T(8,128)(2,1)S(1)}, bf16[2,64,128]{2,1,0:T(8,128)(2,1)S(1)}, u32[]{:S(2)}, u32[]{:S(2)}) %collective-permute-start) | collective-permute-done | bytes 32800 | tf_op jit(solution)/shard_map/ppermute | solution.py:323
  22.1 0.0 collective-permute-done.1.refs_4_
  22.1 0.7 copy-done.9
  22.8 0.7 copy-done.12
  23.5 5.7 %cell_product.2 = (f32[32,64,128]{2,1,0:T(8,128)S(1)}, bf16[32,64,128]{2,1,0:T(8,128)(2,1)}) custom-call(s32[3,16]{1,0:T(4,128)S(1)} %bitcast.7, s32[16]{0:T(128)S(1)} %copy-done.12, bf16[2,64,128]{2,1,0:T(8,128)(2,1)S(1)} %collective-permute-done.refs_2_, bf16[32,64,128]{2,1,0:T(8,128)(2,1)} %get-tuple-element.19.refs_3_, ...), custom_call_target="tpu_custom_call" | custom-call | flops 402653184 | bytes 9437184 | tf_op jit(solution)/shard_map/cell_product/pallas_call | solution.py:162
  29.1 1.0 copy-done.4
  30.1 1.4 %all-to-all-done.mine_ref = bf16[32,64,128]{2,1,0:T(8,128)(2,1)S(1)} async-done(((bf16[32,64,128]{2,1,0:T(8,128)(2,1)}), bf16[32,64,128]{2,1,0:T(8,128)(2,1)S(1)}, u32[]{:S(2)}, u32[]{:S(2)}) %all-to-all-start) | async-done | bytes 524320 | tf_op jit(solution)/shard_map/all_to_all | solution.py:314
  31.5 8.5 %all-to-all-start.2 = ((bf16[32,64,128]{2,1,0:T(8,128)(2,1)}), bf16[32,64,128]{2,1,0:T(8,128)(2,1)S(1)}, u32[]{:S(2)}, u32[]{:S(2)}) async-start(bf16[32,64,128]{2,1,0:T(8,128)(2,1)} %get-tuple-element.28), calls=%async_computation.2 | async-start | bytes 1048576 | tf_op jit(solution)/shard_map/all_to_all | solution.py:314
  40.0 0.1 collective-permute-start.2
  40.1 0.0 copy-start.2
  40.1 1.9 %copy-done.2 = bf16[32,3,128,128]{3,2,1,0:T(8,128)(2,1)S(1)} copy-done((bf16[32,3,128,128]{3,2,1,0:T(8,128)(2,1)S(1)}, bf16[32,3,128,128]{3,2,1,0:T(8,128)(2,1)}, u32[]{:S(2)}) %copy-start.2) | copy-done | bytes 3145752
  42.0 1.4 %turn_tiles.1.turned_ref = bf16[32,64,384]{2,1,0:T(8,128)(2,1)S(1)} custom-call(bf16[32,3,128,128]{3,2,1,0:T(8,128)(2,1)S(1)} %copy-done.2), custom_call_target="tpu_custom_call" | custom-call | flops 16777216 | bytes 5242880 | tf_op jit(solution)/shard_map/turn_tiles/pallas_call | solution.py:200
  43.4 0.0 collective-permute-done.2.other_ref
  43.4 0.0 copy-done.11
  43.4 1.5 %first_gene.1 = (bf16[32,64,128]{2,1,0:T(8,128)(2,1)S(1)}, f32[32,64,128]{2,1,0:T(8,128)S(1)}) custom-call(s32[3,32]{1,0:T(4,128)S(1)} %bitcast.9, bf16[32,64,384]{2,1,0:T(8,128)(2,1)S(1)} %turn_tiles.1.turned_ref, bf16[32,64,128]{2,1,0:T(8,128)(2,1)S(1)} %all-to-all-done.mine_ref, bf16[32,64,128]{2,1,0:T(8,128)(2,1)S(1)} %collective-permute-done.2.other_ref), custom_call_target="tpu_custom_call" | custom-call | flops 201326592 | bytes 5242880 | tf_op jit(solution)/shard_map/first_gene/pallas_call | solution.py:233
  44.9 0.0 copy-start.6
  44.9 1.0 %copy-done.6 = f32[32,64,128]{2,1,0:T(8,128)} copy-done((f32[32,64,128]{2,1,0:T(8,128)}, f32[32,64,128]{2,1,0:T(8,128)S(1)}, u32[]{:S(2)}) %copy-start.6) | copy-done | bytes 1048600
  45.9 0.8 copy-done.8
  46.7 9.3 %all-to-all-done.2.cell_ref = bf16[32,64,128]{2,1,0:T(8,128)(2,1)S(1)} async-done(((bf16[32,64,128]{2,1,0:T(8,128)(2,1)}), bf16[32,64,128]{2,1,0:T(8,128)(2,1)S(1)}, u32[]{:S(2)}, u32[]{:S(2)}) %all-to-all-start.2) | async-done | bytes 524320 | tf_op jit(solution)/shard_map/all_to_all | solution.py:314
  56.0 4.8 %all-to-all-start.1 = ((bf16[32,64,128]{2,1,0:T(8,128)(2,1)}), bf16[32,64,128]{2,1,0:T(8,128)(2,1)S(1)}, u32[]{:S(2)}, u32[]{:S(2)}) async-start(bf16[32,64,128]{2,1,0:T(8,128)(2,1)} %copy-done.8), calls=%async_computation.1 | async-start | bytes 1048576 | tf_op jit(solution)/shard_map/all_to_all | solution.py:314
  60.8 0.0 copy-start.7
  60.8 1.2 %copy-done.7 = f32[32,64,128]{2,1,0:T(8,128)S(1)} copy-done((f32[32,64,128]{2,1,0:T(8,128)S(1)}, f32[32,64,128]{2,1,0:T(8,128)}, u32[]{:S(2)}) %copy-start.7) | copy-done | bytes 1048600
  62.0 0.4 move_rows.1
  62.5 0.0 copy-start.1
  62.5 0.1 collective-permute-start.5
  62.6 1.9 %collective-permute-done.5.other_ref = bf16[32,64,128]{2,1,0:T(8,128)(2,1)S(1)} collective-permute-done((bf16[32,64,128]{2,1,0:T(8,128)(2,1)S(1)}, bf16[32,64,128]{2,1,0:T(8,128)(2,1)S(1)}, u32[]{:S(2)}, u32[]{:S(2)}) %collective-permute-start.5) | collective-permute-done | bytes 524320 | tf_op jit(solution)/shard_map/ppermute | solution.py:318
  64.5 1.5 %second_gene.1 = bf16[32,64,128]{2,1,0:T(8,128)(2,1)S(1)} custom-call(s32[3,32]{1,0:T(4,128)S(1)} %bitcast.10, bf16[32,64,384]{2,1,0:T(8,128)(2,1)S(1)} %turn_tiles.1.turned_ref, bf16[32,64,128]{2,1,0:T(8,128)(2,1)S(1)} %get-tuple-element.29.mine_ref, bf16[32,64,128]{2,1,0:T(8,128)(2,1)S(1)} %collective-permute-done.5.other_ref, ...), custom_call_target="tpu_custom_call" | custom-call | flops 201326592 | bytes 5242880 | tf_op jit(solution)/shard_map/second_gene/pallas_call | solution.py:274
  66.0 0.0 copy-start.3
  66.0 0.8 copy-done.3
  66.8 9.3 %all-to-all-done.1.gene_ref = bf16[32,64,128]{2,1,0:T(8,128)(2,1)S(1)} async-done(((bf16[32,64,128]{2,1,0:T(8,128)(2,1)}), bf16[32,64,128]{2,1,0:T(8,128)(2,1)S(1)}, u32[]{:S(2)}, u32[]{:S(2)}) %all-to-all-start.1) | async-done | bytes 524320 | tf_op jit(solution)/shard_map/all_to_all | solution.py:314
  76.1 4.8 %all-to-all-start.3 = ((bf16[32,64,128]{2,1,0:T(8,128)(2,1)}), bf16[32,64,128]{2,1,0:T(8,128)(2,1)S(1)}, u32[]{:S(2)}, u32[]{:S(2)}) async-start(bf16[32,64,128]{2,1,0:T(8,128)(2,1)} %copy-done.3), calls=%async_computation.3 | async-start | bytes 1048576 | tf_op jit(solution)/shard_map/all_to_all | solution.py:314
  80.9 0.0 copy-done.1
  81.0 0.0 copy-start.5
  81.0 1.2 %copy-done.5 = f32[32,64,128]{2,1,0:T(8,128)S(1)} copy-done((f32[32,64,128]{2,1,0:T(8,128)S(1)}, f32[32,64,128]{2,1,0:T(8,128)}, u32[]{:S(2)}) %copy-start.5) | copy-done | bytes 1048600
  82.2 0.4 move_chunks.1
  82.6 0.7 collective-permute-start.4
  83.3 1.4 %collective-permute-start.3 = (bf16[2,64,128]{2,1,0:T(8,128)(2,1)S(1)}, bf16[2,64,128]{2,1,0:T(8,128)(2,1)S(1)}, u32[]{:S(2)}, u32[]{:S(2)}) collective-permute-start(bf16[2,64,128]{2,1,0:T(8,128)(2,1)S(1)} %get-tuple-element.23), channel_id=1, source_target_pairs={{0,64},{64,128},{128,192},{192,0},{1,65},{65,129},{129,193},{193,1... | collective-permute-start | bytes 98312 | tf_op jit(solution)/shard_map/ppermute | solution.py:323
  84.7 3.7 %collective-permute-done.3.refs_2_ = bf16[2,64,128]{2,1,0:T(8,128)(2,1)S(1)} collective-permute-done((bf16[2,64,128]{2,1,0:T(8,128)(2,1)S(1)}, bf16[2,64,128]{2,1,0:T(8,128)(2,1)S(1)}, u32[]{:S(2)}, u32[]{:S(2)}) %collective-permute-start.3) | collective-permute-done | bytes 32800 | tf_op jit(solution)/shard_map/ppermute | solution.py:323
  88.4 0.0 collective-permute-done.4.refs_4_
  88.4 0.0 copy-done.13
  88.4 4.9 %cell_product.3.near_ref = f32[32,64,128]{2,1,0:T(8,128)S(1)} custom-call(s32[3,16]{1,0:T(4,128)S(1)} %bitcast.8, s32[16]{0:T(128)S(1)} %copy-done.13, bf16[2,64,128]{2,1,0:T(8,128)(2,1)S(1)} %collective-permute-done.3.refs_2_, bf16[32,64,128]{2,1,0:T(8,128)(2,1)S(1)} %get-tuple-element.24.refs_3_, bf16[4,64,128]{2,1,0:T(8,128)(2,1)S(1)} %collective-permute-done.4.refs_4_, ...), custom_call_target="tpu_custom_call" | custom-call | flops 402653184 | bytes 9437184 | tf_op jit(solution)/shard_map/cell_product/pallas_call | solution.py:162
  93.3 2.5 %all-to-all-done.3.gene_ref = bf16[32,64,128]{2,1,0:T(8,128)(2,1)S(1)} async-done(((bf16[32,64,128]{2,1,0:T(8,128)(2,1)}), bf16[32,64,128]{2,1,0:T(8,128)(2,1)S(1)}, u32[]{:S(2)}, u32[]{:S(2)}) %all-to-all-start.3) | async-done | bytes 524320 | tf_op jit(solution)/shard_map/all_to_all | solution.py:314
  95.8 1.0 %last_step.1 = f32[64,4096]{1,0:T(8,128)} custom-call(f32[64,4096]{1,0:T(8,128)S(1)} %bitcast.6, f32[32,64,128]{2,1,0:T(8,128)S(1)} %cell_product.3.near_ref, bf16[32,64,128]{2,1,0:T(8,128)(2,1)S(1)} %all-to-all-done.3.gene_ref), custom_call_target="tpu_custom_call" | custom-call | flops 1048576 | bytes 4194304 | tf_op jit(solution)/shard_map/last_step/pallas_call | solution.py:301
  (9 shorter events, 0.0 us)
Async XLA Ops:
  0.0 1.2 %copy-start = (f32[4096,64]{0,1:T(8,128)S(1)}, f32[4096,64]{0,1:T(8,128)}, u32[]{:S(2)}) copy-start(f32[4096,64]{0,1:T(8,128)} %param.6) | copy-start | bytes 3145732
  2.7 28.8 %all-to-all-start = ((bf16[32,64,128]{2,1,0:T(8,128)(2,1)}), bf16[32,64,128]{2,1,0:T(8,128)(2,1)S(1)}, u32[]{:S(2)}, u32[]{:S(2)}) async-start(bf16[32,64,128]{2,1,0:T(8,128)(2,1)} %get-tuple-element.19.refs_3_), calls=%async_computation | async-start | bytes 1048576 | tf_op jit(solution)/shard_map/all_to_all | solution.py:314
  13.9 8.2 %collective-permute-start.1 = (bf16[4,64,128]{2,1,0:T(8,128)(2,1)S(1)}, bf16[4,64,128]{2,1,0:T(8,128)(2,1)S(1)}, u32[]{:S(2)}, u32[]{:S(2)}) collective-permute-start(bf16[4,64,128]{2,1,0:T(8,128)(2,1)S(1)} %get-tuple-element.20), channel_id=1, source_target_pairs={{64,0},{128,64},{192,128},{0,192},{65,1},{129,65},{193,129},{1,193... | collective-permute-start | bytes 196616 | tf_op jit(solution)/shard_map/ppermute | solution.py:324
  17.0 5.1 %collective-permute-start = (bf16[2,64,128]{2,1,0:T(8,128)(2,1)S(1)}, bf16[2,64,128]{2,1,0:T(8,128)(2,1)S(1)}, u32[]{:S(2)}, u32[]{:S(2)}) collective-permute-start(bf16[2,64,128]{2,1,0:T(8,128)(2,1)S(1)} %get-tuple-element.18), channel_id=1, source_target_pairs={{0,64},{64,128},{128,192},{192,0},{1,65},{65,129},{129,193},{193,1... | collective-permute-start | bytes 98312 | tf_op jit(solution)/shard_map/ppermute | solution.py:323
  22.1 0.7 copy-start.9
  22.8 0.7 copy-start.12
  29.1 1.0 %copy-start.4 = (f32[32,64,128]{2,1,0:T(8,128)}, f32[32,64,128]{2,1,0:T(8,128)S(1)}, u32[]{:S(2)}) copy-start(f32[32,64,128]{2,1,0:T(8,128)S(1)} %get-tuple-element.21.cell_ref) | copy-start | bytes 3145732
  30.1 13.3 %copy-start.11 = (s32[32,3]{0,1:T(4,128)S(1)}, s32[32,3]{0,1:T(4,128)}, u32[]{:S(2)}) copy-start(s32[32,3]{0,1:T(4,128)} %param.11) | copy-start | bytes 1156
  31.5 24.4 %all-to-all-start.2 = ((bf16[32,64,128]{2,1,0:T(8,128)(2,1)}), bf16[32,64,128]{2,1,0:T(8,128)(2,1)S(1)}, u32[]{:S(2)}, u32[]{:S(2)}) async-start(bf16[32,64,128]{2,1,0:T(8,128)(2,1)} %get-tuple-element.28), calls=%async_computation.2 | async-start | bytes 1048576 | tf_op jit(solution)/shard_map/all_to_all | solution.py:314
  40.0 3.4 %collective-permute-start.2 = (bf16[32,64,128]{2,1,0:T(8,128)(2,1)S(1)}, bf16[32,64,128]{2,1,0:T(8,128)(2,1)S(1)}, u32[]{:S(2)}, u32[]{:S(2)}) collective-permute-start(bf16[32,64,128]{2,1,0:T(8,128)(2,1)S(1)} %all-to-all-done.mine_ref), channel_id=1, source_target_pairs={{0,1},{1,0},{2,3},{3,2},{4,5},{5,4},{6,7},{7,6},{8,9},{9,8},{10,11... | collective-permute-start | bytes 1572872 | tf_op jit(solution)/shard_map/ppermute | solution.py:318
  40.1 1.9 %copy-start.2 = (bf16[32,3,128,128]{3,2,1,0:T(8,128)(2,1)S(1)}, bf16[32,3,128,128]{3,2,1,0:T(8,128)(2,1)}, u32[]{:S(2)}) copy-start(bf16[32,3,128,128]{3,2,1,0:T(8,128)(2,1)} %tiles_ref.1) | copy-start | bytes 9437188
  44.9 1.0 %copy-start.6 = (f32[32,64,128]{2,1,0:T(8,128)}, f32[32,64,128]{2,1,0:T(8,128)S(1)}, u32[]{:S(2)}) copy-start(f32[32,64,128]{2,1,0:T(8,128)S(1)} %get-tuple-element.27.gene_ref) | copy-start | bytes 3145732
  45.9 0.8 copy-start.8
  56.0 20.1 %all-to-all-start.1 = ((bf16[32,64,128]{2,1,0:T(8,128)(2,1)}), bf16[32,64,128]{2,1,0:T(8,128)(2,1)S(1)}, u32[]{:S(2)}, u32[]{:S(2)}) async-start(bf16[32,64,128]{2,1,0:T(8,128)(2,1)} %copy-done.8), calls=%async_computation.1 | async-start | bytes 1048576 | tf_op jit(solution)/shard_map/all_to_all | solution.py:314
  60.8 1.2 %copy-start.7 = (f32[32,64,128]{2,1,0:T(8,128)S(1)}, f32[32,64,128]{2,1,0:T(8,128)}, u32[]{:S(2)}) copy-start(f32[32,64,128]{2,1,0:T(8,128)} %copy-done.6) | copy-start | bytes 3145732
  62.5 18.5 %copy-start.1 = (f32[4096,64]{0,1:T(8,128)S(1)}, f32[4096,64]{0,1:T(8,128)}, u32[]{:S(2)}) copy-start(f32[4096,64]{0,1:T(8,128)} %param.6) | copy-start | bytes 3145732
  62.5 2.0 %collective-permute-start.5 = (bf16[32,64,128]{2,1,0:T(8,128)(2,1)S(1)}, bf16[32,64,128]{2,1,0:T(8,128)(2,1)S(1)}, u32[]{:S(2)}, u32[]{:S(2)}) collective-permute-start(bf16[32,64,128]{2,1,0:T(8,128)(2,1)S(1)} %get-tuple-element.29.mine_ref), channel_id=1, source_target_pairs={{0,1},{1,0},{2,3},{3,2},{4,5},{5,4},{6,7},{7,6},{8,9},{9,8},{10,11... | collective-permute-start | bytes 1572872 | tf_op jit(solution)/shard_map/ppermute | solution.py:318
  64.5 23.9 %copy-start.10 = (s32[16,3]{0,1:T(4,128)S(1)}, s32[16,3]{0,1:T(4,128)}, u32[]{:S(2)}) copy-start(s32[16,3]{0,1:T(4,128)} %param.8) | copy-start | bytes 580
  64.5 23.9 %copy-start.13 = (s32[16]{0:T(128)S(1)}, s32[16]{0:T(128)}, u32[]{:S(2)}) copy-start(s32[16]{0:T(128)} %refs_1_.3) | copy-start | bytes 196
  66.0 0.8 copy-start.3
  76.1 19.7 %all-to-all-start.3 = ((bf16[32,64,128]{2,1,0:T(8,128)(2,1)}), bf16[32,64,128]{2,1,0:T(8,128)(2,1)S(1)}, u32[]{:S(2)}, u32[]{:S(2)}) async-start(bf16[32,64,128]{2,1,0:T(8,128)(2,1)} %copy-done.3), calls=%async_computation.3 | async-start | bytes 1048576 | tf_op jit(solution)/shard_map/all_to_all | solution.py:314
  81.0 1.2 %copy-start.5 = (f32[32,64,128]{2,1,0:T(8,128)S(1)}, f32[32,64,128]{2,1,0:T(8,128)}, u32[]{:S(2)}) copy-start(f32[32,64,128]{2,1,0:T(8,128)} %copy-done.4) | copy-start | bytes 3145732
  82.6 5.8 %collective-permute-start.4 = (bf16[4,64,128]{2,1,0:T(8,128)(2,1)S(1)}, bf16[4,64,128]{2,1,0:T(8,128)(2,1)S(1)}, u32[]{:S(2)}, u32[]{:S(2)}) collective-permute-start(bf16[4,64,128]{2,1,0:T(8,128)(2,1)S(1)} %get-tuple-element.25), channel_id=1, source_target_pairs={{64,0},{128,64},{192,128},{0,192},{65,1},{129,65},{193,129},{1,193... | collective-permute-start | bytes 196616 | tf_op jit(solution)/shard_map/ppermute | solution.py:324
  83.3 5.1 %collective-permute-start.3 = (bf16[2,64,128]{2,1,0:T(8,128)(2,1)S(1)}, bf16[2,64,128]{2,1,0:T(8,128)(2,1)S(1)}, u32[]{:S(2)}, u32[]{:S(2)}) collective-permute-start(bf16[2,64,128]{2,1,0:T(8,128)(2,1)S(1)} %get-tuple-element.23), channel_id=1, source_target_pairs={{0,64},{64,128},{128,192},{192,0},{1,65},{65,129},{129,193},{193,1... | collective-permute-start | bytes 98312 | tf_op jit(solution)/shard_map/ppermute | solution.py:323

commit v4 on v3

--- a/solution.py
+++ b/solution.py
@@ -19,6 +19,7 @@
 
 VMEM = pl.BlockSpec(memory_space=pltpu.VMEM)
 SMEM = pl.BlockSpec(memory_space=pltpu.SMEM)
+HBM = pl.BlockSpec(memory_space=pl.ANY)
 CHUNKED = (CHIPS, OWN, CHUNK)
 DIMS_NT = (((1,), (1,)), ((), ()))
 
@@ -60,8 +61,27 @@
     return x_ref[:, j * CHUNK : (j + 1) * CHUNK]
 
 
-def cast_kernel(x_ref, low_ref, head_ref, tail_ref):
-    low_chunks(lambda j: piece(x_ref, j), low_ref, head_ref, tail_ref)
+def cast_kernel(x_ref, low_ref, head_ref, tail_ref, x_held, low_held, in_sems, out_sems):
+    width = PART * CHUNK
+    fetches = [
+        pltpu.make_async_copy(x_ref.at[:, pl.ds(s * width, width)], x_held.at[:, pl.ds(s * width, width)], in_sems.at[s])
+        for s in range(LOWP_STEP)
+    ]
+    for copy in fetches:
+        copy.start()
+    sends = []
+    for s in range(LOWP_STEP):
+        fetches[s].wait()
+        for j in range(s * PART, (s + 1) * PART):
+            low_held[j] = piece(x_held, j).astype(jnp.bfloat16)
+        at = pl.ds(s * PART, PART)
+        send = pltpu.make_async_copy(low_held.at[at], low_ref.at[at], out_sems.at[s])
+        send.start()
+        sends.append(send)
+    head_ref[...] = low_held[: 2 * AFTER]
+    tail_ref[...] = low_held[CHIPS - 2 * BEFORE :]
+    for send in sends:
+        send.wait()
 
 
 def move_kernel(x_ref, cell_ref, gene_ref, low_ref, head_ref, tail_ref, d_ref):
@@ -85,11 +105,16 @@
 def cast_chunks(x):
     return pl.pallas_call(
         cast_kernel,
-        grid=(LOWP_STEP,),
         out_shape=LOW_SHAPES,
-        in_specs=[X_BLOCK],
-        out_specs=[PART_BLOCK, VMEM, VMEM],
-        compiler_params=params(8),
+        in_specs=[HBM],
+        out_specs=[HBM, VMEM, VMEM],
+        scratch_shapes=[
+            pltpu.VMEM((OWN, CHIPS * CHUNK), jnp.float32),
+            pltpu.VMEM(CHUNKED, jnp.bfloat16),
+            pltpu.SemaphoreType.DMA((LOWP_STEP,)),
+            pltpu.SemaphoreType.DMA((LOWP_STEP,)),
+        ],
+        compiler_params=params(60),
         cost_estimate=cost(1 << 18, 3 << 19),
         name="cast_chunks",
     )(x)
@@ -108,7 +133,7 @@
     )(x, cell, gene)
 
 
-CELL_STEP = 4
+CELL_STEP = 8
 CELL_MIB = 48
 
 

time: 98.2 us -> 97.8 us (level)
    pallas_call x2, Pallas kernels: 10.5 us -> 8.95 us  [cell_product(): pl.pallas_call(kernel, grid=(BLOCKS // CELL_STEP,), out_shape=[jax.ShapeD...]
    pallas_call x1, Pallas kernels: 1.47 us -> 2.58 us  [cast_chunks(): pl.pallas_call(cast_kernel, out_shape=LOW_SHAPES, in_specs=[HBM], out_spe...]
  transfers between devices with their start and end apart: 10 -> 10, of which waited for: 7 -> 7; matrix products, arithmetic and copies ran while one was open for 0% -> 0% of each run, Pallas kernels for 16% -> 15%
where the time goes in v4:
time: 97.8 us; the launch traced here: 97.1 us
  starting transfers between devices  35.2 us (36%)
  waiting for transfers between devices  33.7 us (34%)
  Pallas kernels  17.8 us (18%)
  local copies, waits for them, and re-layouts  10.3 us (11%)
    all_to_all x4, starting transfers between devices, exchange(): lax.all_to_all(chunks, 'chip', split_axis=0, concat_axis=0, tiled=True)  29.8 us
    all_to_all x4, waiting for transfers between devices, exchange(): lax.all_to_all(chunks, 'chip', split_axis=0, concat_axis=0, tiled=True)  22.7 us
    unnamed x28, local copies, waits for them, and re-layouts  10.3 us
    ppermute x2, waiting for transfers between devices, halo(): before = lax.ppermute(tail, 'slab', [(i, (i + 1) % n) for i in range(n)])  9.07 us
    pallas_call x2, Pallas kernels, cell_product(): pl.pallas_call(kernel, grid=(BLOCKS // CELL_STEP,), out_shape=[jax.ShapeD...  8.95 us
    ppermute x2, starting transfers between devices, halo(): after = lax.ppermute(head, 'slab', [((i + 1) % n, i) for i in range(n)])  3.8 us
    pallas_call x1, Pallas kernels, cast_chunks(): pl.pallas_call(cast_kernel, out_shape=LOW_SHAPES, in_specs=[HBM], out_spe...  2.58 us
  transfers between devices with their start and end apart: 10, of which 7 were waited for; matrix products, arithmetic and copies ran while one was open for 0% of the time, Pallas kernels for 15%

profile of v4, /device:TPU:32, one launch (start us, length us, event | category | flops | bytes accessed | tf_op | source)
XLA Modules:
  0.0 97.1 jit_solution(3708851526420667632)
XLA Ops:
  0.0 2.6 %cast_chunks.1 = (bf16[32,64,128]{2,1,0:T(8,128)(2,1)}, bf16[4,64,128]{2,1,0:T(8,128)(2,1)}, bf16[2,64,128]{2,1,0:T(8,128)(2,1)}) custom-call(f32[64,4096]{1,0:T(8,128)} %bitcast.4), custom_call_target="tpu_custom_call" | custom-call | flops 262144 | bytes 1572864 | tf_op jit(solution)/shard_map/cast_chunks/pallas_call | solution.py:106
  2.6 11.2 %all-to-all-start = ((bf16[32,64,128]{2,1,0:T(8,128)(2,1)}), bf16[32,64,128]{2,1,0:T(8,128)(2,1)S(1)}, u32[]{:S(2)}, u32[]{:S(2)}) async-start(bf16[32,64,128]{2,1,0:T(8,128)(2,1)} %get-tuple-element.19.refs_3_), calls=%async_computation | async-start | bytes 1048576 | tf_op jit(solution)/shard_map/all_to_all | solution.py:339
  13.8 3.1 %collective-permute-start.1 = (bf16[4,64,128]{2,1,0:T(8,128)(2,1)}, bf16[4,64,128]{2,1,0:T(8,128)(2,1)S(1)}, u32[]{:S(2)}, u32[]{:S(2)}) collective-permute-start(bf16[4,64,128]{2,1,0:T(8,128)(2,1)} %get-tuple-element.20), channel_id=1, source_target_pairs={{64,0},{128,64},{192,128},{0,192},{65,1},{129,65},{193,129},{1,193... | collective-permute-start | bytes 196616 | tf_op jit(solution)/shard_map/ppermute | solution.py:349
  16.9 0.0 collective-permute-start
  16.9 5.3 %collective-permute-done.refs_2_ = bf16[2,64,128]{2,1,0:T(8,128)(2,1)S(1)} collective-permute-done((bf16[2,64,128]{2,1,0:T(8,128)(2,1)}, bf16[2,64,128]{2,1,0:T(8,128)(2,1)S(1)}, u32[]{:S(2)}, u32[]{:S(2)}) %collective-permute-start) | collective-permute-done | bytes 32800 | tf_op jit(solution)/shard_map/ppermute | solution.py:348
  22.2 0.0 collective-permute-done.1.refs_4_
  22.2 1.0 %copy-done.3 = bf16[32,64,128]{2,1,0:T(8,128)(2,1)S(1)} copy-done((bf16[32,64,128]{2,1,0:T(8,128)(2,1)S(1)}, bf16[32,64,128]{2,1,0:T(8,128)(2,1)}, u32[]{:S(2)}) %copy-start.3) | copy-done | bytes 524312
  23.3 0.7 copy-done.9
  24.0 0.7 copy-done.12
  24.6 4.8 %cell_product.2 = (f32[32,64,128]{2,1,0:T(8,128)S(1)}, bf16[32,64,128]{2,1,0:T(8,128)(2,1)}) custom-call(s32[3,16]{1,0:T(4,128)S(1)} %bitcast.7, s32[16]{0:T(128)S(1)} %copy-done.12, bf16[2,64,128]{2,1,0:T(8,128)(2,1)S(1)} %collective-permute-done.refs_2_, bf16[32,64,128]{2,1,0:T(8,128)(2,1)S(1)} %copy-done.3, ...), custom_call_target="tpu_custom_call" | custom-call | flops 402653184 | bytes 9437184 | tf_op jit(solution)/shard_map/cell_product/pallas_call | solution.py:187
  29.4 1.0 copy-done.4
  30.4 1.0 %all-to-all-done.mine_ref = bf16[32,64,128]{2,1,0:T(8,128)(2,1)S(1)} async-done(((bf16[32,64,128]{2,1,0:T(8,128)(2,1)}), bf16[32,64,128]{2,1,0:T(8,128)(2,1)S(1)}, u32[]{:S(2)}, u32[]{:S(2)}) %all-to-all-start) | async-done | bytes 524320 | tf_op jit(solution)/shard_map/all_to_all | solution.py:339
  31.4 8.9 %all-to-all-start.2 = ((bf16[32,64,128]{2,1,0:T(8,128)(2,1)}), bf16[32,64,128]{2,1,0:T(8,128)(2,1)S(1)}, u32[]{:S(2)}, u32[]{:S(2)}) async-start(bf16[32,64,128]{2,1,0:T(8,128)(2,1)} %get-tuple-element.28), calls=%async_computation.2 | async-start | bytes 1048576 | tf_op jit(solution)/shard_map/all_to_all | solution.py:339
  40.3 0.1 collective-permute-start.2
  40.4 0.0 copy-start.1
  40.4 1.9 %copy-done.1 = bf16[32,3,128,128]{3,2,1,0:T(8,128)(2,1)S(1)} copy-done((bf16[32,3,128,128]{3,2,1,0:T(8,128)(2,1)S(1)}, bf16[32,3,128,128]{3,2,1,0:T(8,128)(2,1)}, u32[]{:S(2)}) %copy-start.1) | copy-done | bytes 3145752
  42.3 1.4 %turn_tiles.1.turned_ref = bf16[32,64,384]{2,1,0:T(8,128)(2,1)S(1)} custom-call(bf16[32,3,128,128]{3,2,1,0:T(8,128)(2,1)S(1)} %copy-done.1), custom_call_target="tpu_custom_call" | custom-call | flops 16777216 | bytes 5242880 | tf_op jit(solution)/shard_map/turn_tiles/pallas_call | solution.py:225
  43.7 0.0 collective-permute-done.2.other_ref
  43.7 0.0 copy-done.11
  43.7 1.5 %first_gene.1 = (bf16[32,64,128]{2,1,0:T(8,128)(2,1)S(1)}, f32[32,64,128]{2,1,0:T(8,128)S(1)}) custom-call(s32[3,32]{1,0:T(4,128)S(1)} %bitcast.9, bf16[32,64,384]{2,1,0:T(8,128)(2,1)S(1)} %turn_tiles.1.turned_ref, bf16[32,64,128]{2,1,0:T(8,128)(2,1)S(1)} %all-to-all-done.mine_ref, bf16[32,64,128]{2,1,0:T(8,128)(2,1)S(1)} %collective-permute-done.2.other_ref), custom_call_target="tpu_custom_call" | custom-call | flops 201326592 | bytes 5242880 | tf_op jit(solution)/shard_map/first_gene/pallas_call | solution.py:258
  45.2 0.0 copy-start.6
  45.2 1.0 copy-done.6
  46.2 0.8 copy-done.8
  47.0 9.3 %all-to-all-done.2.cell_ref = bf16[32,64,128]{2,1,0:T(8,128)(2,1)S(1)} async-done(((bf16[32,64,128]{2,1,0:T(8,128)(2,1)}), bf16[32,64,128]{2,1,0:T(8,128)(2,1)S(1)}, u32[]{:S(2)}, u32[]{:S(2)}) %all-to-all-start.2) | async-done | bytes 524320 | tf_op jit(solution)/shard_map/all_to_all | solution.py:339
  56.3 4.8 %all-to-all-start.1 = ((bf16[32,64,128]{2,1,0:T(8,128)(2,1)}), bf16[32,64,128]{2,1,0:T(8,128)(2,1)S(1)}, u32[]{:S(2)}, u32[]{:S(2)}) async-start(bf16[32,64,128]{2,1,0:T(8,128)(2,1)} %copy-done.8), calls=%async_computation.1 | async-start | bytes 1048576 | tf_op jit(solution)/shard_map/all_to_all | solution.py:339
  61.1 0.0 copy-start.7
  61.1 1.2 %copy-done.7 = f32[32,64,128]{2,1,0:T(8,128)S(1)} copy-done((f32[32,64,128]{2,1,0:T(8,128)S(1)}, f32[32,64,128]{2,1,0:T(8,128)}, u32[]{:S(2)}) %copy-start.7) | copy-done | bytes 1048600
  62.3 0.4 move_rows.1
  62.8 0.0 copy-start
  62.8 0.1 collective-permute-start.5
  62.9 1.9 %collective-permute-done.5.other_ref = bf16[32,64,128]{2,1,0:T(8,128)(2,1)S(1)} collective-permute-done((bf16[32,64,128]{2,1,0:T(8,128)(2,1)S(1)}, bf16[32,64,128]{2,1,0:T(8,128)(2,1)S(1)}, u32[]{:S(2)}, u32[]{:S(2)}) %collective-permute-start.5) | collective-permute-done | bytes 524320 | tf_op jit(solution)/shard_map/ppermute | solution.py:343
  64.8 1.5 %second_gene.1 = bf16[32,64,128]{2,1,0:T(8,128)(2,1)S(1)} custom-call(s32[3,32]{1,0:T(4,128)S(1)} %bitcast.10, bf16[32,64,384]{2,1,0:T(8,128)(2,1)S(1)} %turn_tiles.1.turned_ref, bf16[32,64,128]{2,1,0:T(8,128)(2,1)S(1)} %get-tuple-element.29.mine_ref, bf16[32,64,128]{2,1,0:T(8,128)(2,1)S(1)} %collective-permute-done.5.other_ref, ...), custom_call_target="tpu_custom_call" | custom-call | flops 201326592 | bytes 5242880 | tf_op jit(solution)/shard_map/second_gene/pallas_call | solution.py:299
  66.3 0.0 copy-start.2
  66.3 0.8 copy-done.2
  67.1 9.3 %all-to-all-done.1.gene_ref = bf16[32,64,128]{2,1,0:T(8,128)(2,1)S(1)} async-done(((bf16[32,64,128]{2,1,0:T(8,128)(2,1)}), bf16[32,64,128]{2,1,0:T(8,128)(2,1)S(1)}, u32[]{:S(2)}, u32[]{:S(2)}) %all-to-all-start.1) | async-done | bytes 524320 | tf_op jit(solution)/shard_map/all_to_all | solution.py:339
  76.4 4.8 %all-to-all-start.3 = ((bf16[32,64,128]{2,1,0:T(8,128)(2,1)}), bf16[32,64,128]{2,1,0:T(8,128)(2,1)S(1)}, u32[]{:S(2)}, u32[]{:S(2)}) async-start(bf16[32,64,128]{2,1,0:T(8,128)(2,1)} %copy-done.2), calls=%async_computation.3 | async-start | bytes 1048576 | tf_op jit(solution)/shard_map/all_to_all | solution.py:339
  81.3 0.0 copy-done
  81.3 0.0 copy-start.5
  81.3 1.2 %copy-done.5 = f32[32,64,128]{2,1,0:T(8,128)S(1)} copy-done((f32[32,64,128]{2,1,0:T(8,128)S(1)}, f32[32,64,128]{2,1,0:T(8,128)}, u32[]{:S(2)}) %copy-start.5) | copy-done | bytes 1048600
  82.5 0.4 move_chunks.1
  82.9 0.7 collective-permute-start.4
  83.6 1.4 %collective-permute-start.3 = (bf16[2,64,128]{2,1,0:T(8,128)(2,1)S(1)}, bf16[2,64,128]{2,1,0:T(8,128)(2,1)S(1)}, u32[]{:S(2)}, u32[]{:S(2)}) collective-permute-start(bf16[2,64,128]{2,1,0:T(8,128)(2,1)S(1)} %get-tuple-element.23), channel_id=1, source_target_pairs={{0,64},{64,128},{128,192},{192,0},{1,65},{65,129},{129,193},{193,1... | collective-permute-start | bytes 98312 | tf_op jit(solution)/shard_map/ppermute | solution.py:348
  85.0 3.7 %collective-permute-done.3.refs_2_ = bf16[2,64,128]{2,1,0:T(8,128)(2,1)S(1)} collective-permute-done((bf16[2,64,128]{2,1,0:T(8,128)(2,1)S(1)}, bf16[2,64,128]{2,1,0:T(8,128)(2,1)S(1)}, u32[]{:S(2)}, u32[]{:S(2)}) %collective-permute-start.3) | collective-permute-done | bytes 32800 | tf_op jit(solution)/shard_map/ppermute | solution.py:348
  88.7 0.0 collective-permute-done.4.refs_4_
  88.7 0.0 copy-done.13
  88.7 4.1 %cell_product.3.near_ref = f32[32,64,128]{2,1,0:T(8,128)S(1)} custom-call(s32[3,16]{1,0:T(4,128)S(1)} %bitcast.8, s32[16]{0:T(128)S(1)} %copy-done.13, bf16[2,64,128]{2,1,0:T(8,128)(2,1)S(1)} %collective-permute-done.3.refs_2_, bf16[32,64,128]{2,1,0:T(8,128)(2,1)S(1)} %get-tuple-element.24.refs_3_, bf16[4,64,128]{2,1,0:T(8,128)(2,1)S(1)} %collective-permute-done.4.refs_4_, ...), custom_call_target="tpu_custom_call" | custom-call | flops 402653184 | bytes 9437184 | tf_op jit(solution)/shard_map/cell_product/pallas_call | solution.py:187
  92.9 3.2 %all-to-all-done.3.gene_ref = bf16[32,64,128]{2,1,0:T(8,128)(2,1)S(1)} async-done(((bf16[32,64,128]{2,1,0:T(8,128)(2,1)}), bf16[32,64,128]{2,1,0:T(8,128)(2,1)S(1)}, u32[]{:S(2)}, u32[]{:S(2)}) %all-to-all-start.3) | async-done | bytes 524320 | tf_op jit(solution)/shard_map/all_to_all | solution.py:339
  96.1 1.0 %last_step.1 = f32[64,4096]{1,0:T(8,128)} custom-call(f32[64,4096]{1,0:T(8,128)S(1)} %bitcast.6, f32[32,64,128]{2,1,0:T(8,128)S(1)} %cell_product.3.near_ref, bf16[32,64,128]{2,1,0:T(8,128)(2,1)S(1)} %all-to-all-done.3.gene_ref), custom_call_target="tpu_custom_call" | custom-call | flops 1048576 | bytes 4194304 | tf_op jit(solution)/shard_map/last_step/pallas_call | solution.py:326
  (9 shorter events, 0.0 us)
Async XLA Ops:
  2.6 28.8 %all-to-all-start = ((bf16[32,64,128]{2,1,0:T(8,128)(2,1)}), bf16[32,64,128]{2,1,0:T(8,128)(2,1)S(1)}, u32[]{:S(2)}, u32[]{:S(2)}) async-start(bf16[32,64,128]{2,1,0:T(8,128)(2,1)} %get-tuple-element.19.refs_3_), calls=%async_computation | async-start | bytes 1048576 | tf_op jit(solution)/shard_map/all_to_all | solution.py:339
  13.8 8.4 %collective-permute-start.1 = (bf16[4,64,128]{2,1,0:T(8,128)(2,1)}, bf16[4,64,128]{2,1,0:T(8,128)(2,1)S(1)}, u32[]{:S(2)}, u32[]{:S(2)}) collective-permute-start(bf16[4,64,128]{2,1,0:T(8,128)(2,1)} %get-tuple-element.20), channel_id=1, source_target_pairs={{64,0},{128,64},{192,128},{0,192},{65,1},{129,65},{193,129},{1,193... | collective-permute-start | bytes 196616 | tf_op jit(solution)/shard_map/ppermute | solution.py:349
  16.9 5.3 %collective-permute-start = (bf16[2,64,128]{2,1,0:T(8,128)(2,1)}, bf16[2,64,128]{2,1,0:T(8,128)(2,1)S(1)}, u32[]{:S(2)}, u32[]{:S(2)}) collective-permute-start(bf16[2,64,128]{2,1,0:T(8,128)(2,1)} %get-tuple-element.18), channel_id=1, source_target_pairs={{0,64},{64,128},{128,192},{192,0},{1,65},{65,129},{129,193},{193,1... | collective-permute-start | bytes 98312 | tf_op jit(solution)/shard_map/ppermute | solution.py:348
  22.2 1.0 %copy-start.3 = (bf16[32,64,128]{2,1,0:T(8,128)(2,1)S(1)}, bf16[32,64,128]{2,1,0:T(8,128)(2,1)}, u32[]{:S(2)}) copy-start(bf16[32,64,128]{2,1,0:T(8,128)(2,1)} %get-tuple-element.19.refs_3_) | copy-start | bytes 1572868
  23.3 0.7 copy-start.9
  24.0 0.7 copy-start.12
  29.4 1.0 copy-start.4
  30.4 13.3 %copy-start.11 = (s32[32,3]{0,1:T(4,128)S(1)}, s32[32,3]{0,1:T(4,128)}, u32[]{:S(2)}) copy-start(s32[32,3]{0,1:T(4,128)} %param.11) | copy-start | bytes 1156
  31.4 24.9 %all-to-all-start.2 = ((bf16[32,64,128]{2,1,0:T(8,128)(2,1)}), bf16[32,64,128]{2,1,0:T(8,128)(2,1)S(1)}, u32[]{:S(2)}, u32[]{:S(2)}) async-start(bf16[32,64,128]{2,1,0:T(8,128)(2,1)} %get-tuple-element.28), calls=%async_computation.2 | async-start | bytes 1048576 | tf_op jit(solution)/shard_map/all_to_all | solution.py:339
  40.3 3.4 %collective-permute-start.2 = (bf16[32,64,128]{2,1,0:T(8,128)(2,1)S(1)}, bf16[32,64,128]{2,1,0:T(8,128)(2,1)S(1)}, u32[]{:S(2)}, u32[]{:S(2)}) collective-permute-start(bf16[32,64,128]{2,1,0:T(8,128)(2,1)S(1)} %all-to-all-done.mine_ref), channel_id=1, source_target_pairs={{0,1},{1,0},{2,3},{3,2},{4,5},{5,4},{6,7},{7,6},{8,9},{9,8},{10,11... | collective-permute-start | bytes 1572872 | tf_op jit(solution)/shard_map/ppermute | solution.py:343
  40.4 1.9 %copy-start.1 = (bf16[32,3,128,128]{3,2,1,0:T(8,128)(2,1)S(1)}, bf16[32,3,128,128]{3,2,1,0:T(8,128)(2,1)}, u32[]{:S(2)}) copy-start(bf16[32,3,128,128]{3,2,1,0:T(8,128)(2,1)} %tiles_ref.1) | copy-start | bytes 9437188
  45.2 1.0 %copy-start.6 = (f32[32,64,128]{2,1,0:T(8,128)}, f32[32,64,128]{2,1,0:T(8,128)S(1)}, u32[]{:S(2)}) copy-start(f32[32,64,128]{2,1,0:T(8,128)S(1)} %get-tuple-element.27.gene_ref) | copy-start | bytes 3145732
  46.2 0.8 copy-start.8
  56.3 20.1 %all-to-all-start.1 = ((bf16[32,64,128]{2,1,0:T(8,128)(2,1)}), bf16[32,64,128]{2,1,0:T(8,128)(2,1)S(1)}, u32[]{:S(2)}, u32[]{:S(2)}) async-start(bf16[32,64,128]{2,1,0:T(8,128)(2,1)} %copy-done.8), calls=%async_computation.1 | async-start | bytes 1048576 | tf_op jit(solution)/shard_map/all_to_all | solution.py:339
  61.1 1.2 %copy-start.7 = (f32[32,64,128]{2,1,0:T(8,128)S(1)}, f32[32,64,128]{2,1,0:T(8,128)}, u32[]{:S(2)}) copy-start(f32[32,64,128]{2,1,0:T(8,128)} %copy-done.6) | copy-start | bytes 3145732
  62.8 18.5 %copy-start = (f32[4096,64]{0,1:T(8,128)S(1)}, f32[4096,64]{0,1:T(8,128)}, u32[]{:S(2)}) copy-start(f32[4096,64]{0,1:T(8,128)} %param.6) | copy-start | bytes 3145732
  62.8 2.0 %collective-permute-start.5 = (bf16[32,64,128]{2,1,0:T(8,128)(2,1)S(1)}, bf16[32,64,128]{2,1,0:T(8,128)(2,1)S(1)}, u32[]{:S(2)}, u32[]{:S(2)}) collective-permute-start(bf16[32,64,128]{2,1,0:T(8,128)(2,1)S(1)} %get-tuple-element.29.mine_ref), channel_id=1, source_target_pairs={{0,1},{1,0},{2,3},{3,2},{4,5},{5,4},{6,7},{7,6},{8,9},{9,8},{10,11... | collective-permute-start | bytes 1572872 | tf_op jit(solution)/shard_map/ppermute | solution.py:343
  64.8 23.9 %copy-start.10 = (s32[16,3]{0,1:T(4,128)S(1)}, s32[16,3]{0,1:T(4,128)}, u32[]{:S(2)}) copy-start(s32[16,3]{0,1:T(4,128)} %param.8) | copy-start | bytes 580
  64.8 23.9 %copy-start.13 = (s32[16]{0:T(128)S(1)}, s32[16]{0:T(128)}, u32[]{:S(2)}) copy-start(s32[16]{0:T(128)} %refs_1_.3) | copy-start | bytes 196
  66.3 0.8 copy-start.2
  76.4 19.7 %all-to-all-start.3 = ((bf16[32,64,128]{2,1,0:T(8,128)(2,1)}), bf16[32,64,128]{2,1,0:T(8,128)(2,1)S(1)}, u32[]{:S(2)}, u32[]{:S(2)}) async-start(bf16[32,64,128]{2,1,0:T(8,128)(2,1)} %copy-done.2), calls=%async_computation.3 | async-start | bytes 1048576 | tf_op jit(solution)/shard_map/all_to_all | solution.py:339
  81.3 1.2 %copy-start.5 = (f32[32,64,128]{2,1,0:T(8,128)S(1)}, f32[32,64,128]{2,1,0:T(8,128)}, u32[]{:S(2)}) copy-start(f32[32,64,128]{2,1,0:T(8,128)} %copy-done.4) | copy-start | bytes 3145732
  82.9 5.8 %collective-permute-start.4 = (bf16[4,64,128]{2,1,0:T(8,128)(2,1)S(1)}, bf16[4,64,128]{2,1,0:T(8,128)(2,1)S(1)}, u32[]{:S(2)}, u32[]{:S(2)}) collective-permute-start(bf16[4,64,128]{2,1,0:T(8,128)(2,1)S(1)} %get-tuple-element.25), channel_id=1, source_target_pairs={{64,0},{128,64},{192,128},{0,192},{65,1},{129,65},{193,129},{1,193... | collective-permute-start | bytes 196616 | tf_op jit(solution)/shard_map/ppermute | solution.py:349
  83.6 5.1 %collective-permute-start.3 = (bf16[2,64,128]{2,1,0:T(8,128)(2,1)S(1)}, bf16[2,64,128]{2,1,0:T(8,128)(2,1)S(1)}, u32[]{:S(2)}, u32[]{:S(2)}) collective-permute-start(bf16[2,64,128]{2,1,0:T(8,128)(2,1)S(1)} %get-tuple-element.23), channel_id=1, source_target_pairs={{0,64},{64,128},{128,192},{192,0},{1,65},{65,129},{129,193},{193,1... | collective-permute-start | bytes 98312 | tf_op jit(solution)/shard_map/ppermute | solution.py:348
